TPU v7x, 32 devices: a whole 2x2x4 slice. The times are simulated.
32 devices in a mesh: expert: 8 (over y, x, core), shard: 4 (over z).
Axes of the slice: x: 2, y: 2, z: 4, core: 2. Of those that a mesh axis runs over, the one named last changes fastest.
Arguments:
- tokens: bfloat16 [8192, 768], P(('expert', 'shard')), may hold values from -6 to 6
- w_query: bfloat16 [768, 768], P('shard'), may hold values from -0.21875 to 0.21875
- w_key: bfloat16 [768, 768], P('shard'), may hold values from -0.21875 to 0.21875
- w_value: bfloat16 [768, 768], P('shard'), may hold values from -0.21875 to 0.21875
- w_out_attn: bfloat16 [768, 768], P('shard'), may hold values from -2.5 to 2.5
- w_router: bfloat16 [768, 16], P('shard'), may hold values from -0.15625 to 0.15625
- gain_attn: bfloat16 [768], P('shard'), may hold values from 0.5 to 1.5
- gain_moe: bfloat16 [768], P('shard'), may hold values from 0.5 to 1.5
- rel_bias: bfloat16 [32, 12], P('shard'), may hold values from -3 to 3
- w_in: bfloat16 [16, 768, 3072], P('expert', None, 'shard'), may hold values from -0.21875 to 0.21875
- w_out: bfloat16 [16, 3072, 768], P('expert', 'shard'), may hold values from -0.109375 to 0.109375
- out_grad: bfloat16 [8192, 768], P(('expert', 'shard')), may hold values from -6 to 6
- routes: int32 [8192, 2], P(('expert', 'shard')), may hold values from 0 to 15, all different within a row; in each aligned block of 256 rows (0 to 255, 256 to 511, ...) at most 64 rows name the same one
- segments: int32 [8, 1024], P('expert'), may hold values from 0 to 2, as said below
- buckets: int32 [1024], replicated, may hold values from 0 to 31, as said below
Outputs:
- layer_out: bfloat16 [8192, 768], P(('expert', 'shard'))
- tokens_grad: bfloat16 [8192, 768], P(('expert', 'shard'))
- grad_w_query: float32 [768, 768], P('shard')
- grad_w_key: float32 [768, 768], P('shard')
- grad_w_value: float32 [768, 768], P('shard')
- grad_w_out_attn: float32 [768, 768], P('shard')
- grad_w_router: float32 [768, 16], P('shard')
- grad_gain_attn: float32 [768], P('shard')
- grad_gain_moe: float32 [768], P('shard')
- grad_rel_bias: float32 [32, 12], P('shard')
- grad_w_in: float32 [16, 768, 3072], P('expert', None, 'shard')
- grad_w_out: float32 [16, 3072, 768], P('expert', 'shard')
Inputs may be any that keep to these rules, and one draw needn't show every extreme that they name: `routes`: the two experts of a token differ. Among the rows of one device no expert is named by more than 64 rows, a bound that some block reaches. `segments`: document numbers never fall along a sequence; each document is a run of consecutive tokens. Entry d is the bucket of the distance d between a query and an earlier key; buckets never fall as d grows, and distance 0 has bucket 0.
All inputs are finite; a program needn't handle non-finite values.
Results may differ from a plain program's by a relative error of at most 0.025.
Values may be sent and summed in bfloat16 or wider, within the bound.
A program may use at most 128 MiB of HBM per device.

v0:
```python
import math

import jax
import jax.numpy as jnp
from jax import lax
from jax.sharding import PartitionSpec as P

EPSILON = 1e-06
NEG_BIG = -1e30


def matmul(left_operand, right_side):
    return jnp.dot(left_operand, right_side, preferred_element_type=jnp.float32)


def contract_first(left_operand, right_side):
    return lax.dot_general(
        left_operand, right_side, (((0,), (0,)), ((), ())), preferred_element_type=jnp.float32
    )


def contract_last(left_operand, right_side):
    return lax.dot_general(
        left_operand, right_side, (((1,), (1,)), ((), ())), preferred_element_type=jnp.float32
    )


def gelu_slope(pre_act):
    return (
        0.5 * (1.0 + lax.erf(pre_act * 0.7071067811865476))
        + pre_act * jnp.exp(-0.5 * pre_act * pre_act) * 0.3989422804014327
    )


def norm_parts(values, gain_vector):
    inverse = lax.rsqrt(jnp.mean(values * values, axis=-1, keepdims=True) + EPSILON)
    return (values * inverse * gain_vector, inverse)


def norm_back(values, inverse, gain_vector, grad_normed):
    scaled_scores = grad_normed * gain_vector
    grad_gain = jnp.sum(grad_normed * values * inverse, axis=0)
    grad_values = inverse * scaled_scores - values * inverse**3 * jnp.mean(
        scaled_scores * values, axis=-1, keepdims=True
    )
    return (grad_values, grad_gain)


def per_device(
    tokens,
    w_query,
    w_key,
    w_value,
    w_out_attn,
    w_router,
    gain_attn,
    gain_moe,
    rel_bias,
    w_in,
    w_out,
    out_grad,
    routes,
    segments,
    buckets,
):
    gathered = (
        lax.all_gather(w_query, "shard", axis=0, tiled=True),
        lax.all_gather(w_key, "shard", axis=0, tiled=True),
        lax.all_gather(w_value, "shard", axis=0, tiled=True),
        lax.all_gather(w_out_attn, "shard", axis=0, tiled=True),
        lax.all_gather(w_router, "shard", axis=0, tiled=True),
        lax.all_gather(gain_attn, "shard", axis=0, tiled=True),
        lax.all_gather(gain_moe, "shard", axis=0, tiled=True),
        lax.all_gather(rel_bias, "shard", axis=0, tiled=True),
    )
    (
        full_query,
        full_key,
        full_value,
        full_proj,
        full_router,
        gain_one,
        gain_two,
        position_bias_table,
    ) = gathered
    expert_first, expert_second = (
        lax.all_gather(w_in, "shard", axis=2, tiled=True),
        lax.all_gather(w_out, "shard", axis=1, tiled=True),
    )
    rows_here, model_width = tokens.shape
    shard_count = lax.axis_size("shard")
    expert_count = lax.axis_size("expert")
    shard_index = lax.axis_index("shard")
    seq_length = rows_here * shard_count
    head_count = position_bias_table.shape[1]
    head_width = model_width // head_count
    score_scale = head_width ** (-0.5)
    local_experts = w_in.shape[0]
    experts = local_experts * expert_count
    capacity = max(2, 4 * rows_here // experts)
    bucket_count = position_bias_table.shape[0]
    gain_one = gain_one.astype(jnp.float32)
    gain_two = gain_two.astype(jnp.float32)
    inputs = tokens.astype(jnp.float32)
    seq_segments = segments[0]
    query_start = shard_index * rows_here
    local_pos = query_start + jnp.arange(rows_here, dtype=jnp.int32)
    local_seg = lax.dynamic_slice_in_dim(seq_segments, query_start, rows_here, 0)
    bucket_ids = jnp.arange(bucket_count, dtype=jnp.int32)
    bucket_starts = jnp.sum((buckets[None, :] < bucket_ids[:, None]).astype(jnp.int32), axis=1)
    bucket_ends = jnp.concatenate([bucket_starts[1:], jnp.full((1,), seq_length, jnp.int32)])

    def bucket_block(query_pos, key_pos):
        distance = jnp.clip(query_pos[:, None] - key_pos[None, :], 0, seq_length - 1)[None]
        inside = (distance >= bucket_starts[:, None, None]) & (
            distance < bucket_ends[:, None, None]
        )
        return inside.astype(jnp.bfloat16)

    normed_one, inverse_one = norm_parts(inputs, gain_one)
    normed_one = normed_one.astype(jnp.bfloat16)
    queries = matmul(normed_one, full_query).astype(jnp.bfloat16)
    keys_here = matmul(normed_one, full_key).astype(jnp.bfloat16)
    values_here = matmul(normed_one, full_value).astype(jnp.bfloat16)
    query_heads = queries.reshape(rows_here, head_count, head_width)
    start_state = (
        jnp.full((head_count, rows_here), NEG_BIG, jnp.float32),
        jnp.zeros((head_count, rows_here), jnp.float32),
        jnp.zeros((rows_here, head_count, head_width), jnp.float32),
    )
    piece_keys = lax.all_gather(keys_here, "shard", axis=0, tiled=True)
    piece_values = lax.all_gather(values_here, "shard", axis=0, tiled=True)
    piece_rows = piece_keys.shape[0]
    block_rows = math.gcd(piece_rows, 512)

    def step(block_index, loop_state):
        running_max, running_sum, accumulated = loop_state
        offset = block_index * block_rows
        key_block = lax.dynamic_slice_in_dim(piece_keys, offset, block_rows, 0).reshape(
            block_rows, head_count, head_width
        )
        value_block = lax.dynamic_slice_in_dim(piece_values, offset, block_rows, 0).reshape(
            block_rows, head_count, head_width
        )
        key_pos = offset + jnp.arange(block_rows, dtype=jnp.int32)
        key_seg = lax.dynamic_slice_in_dim(seq_segments, offset, block_rows, 0)
        distance_bucket_table = bucket_block(local_pos, key_pos)
        bias_values = jnp.einsum(
            "yoc,yi->ioc",
            distance_bucket_table,
            position_bias_table,
            preferred_element_type=jnp.float32,
        )
        allowed = (
            (local_pos[:, None] >= key_pos[None, :]) & (local_seg[:, None] == key_seg[None, :])
        )[None]
        scores = (
            jnp.einsum("qhd,khd->hqk", query_heads, key_block, preferred_element_type=jnp.float32)
            * score_scale
            + bias_values
        )
        scores = jnp.where(allowed, scores, NEG_BIG)
        new_max = jnp.maximum(running_max, jnp.max(scores, axis=2))
        factor = jnp.exp(running_max - new_max)
        prob_block = jnp.where(allowed, jnp.exp(scores - new_max[:, :, None]), 0.0)
        running_sum = running_sum * factor + jnp.sum(prob_block, axis=2)
        accumulated = accumulated * factor.T[:, :, None] + jnp.einsum(
            "hqk,khd->qhd",
            prob_block.astype(jnp.bfloat16),
            value_block,
            preferred_element_type=jnp.float32,
        )
        return (new_max, running_sum, accumulated)

    final_max, final_sum, accumulated = lax.fori_loop(
        0, piece_rows // block_rows, step, start_state
    )
    head_out = accumulated / final_sum.T[:, :, None]
    log_norm = (final_max + jnp.log(final_sum)).T
    mixed_heads = head_out.reshape(rows_here, model_width).astype(jnp.bfloat16)
    hidden = inputs + matmul(mixed_heads, full_proj)
    normed_two, inverse_two = norm_parts(hidden, gain_two)
    normed_two = normed_two.astype(jnp.bfloat16)
    router = jax.nn.softmax(matmul(normed_two, full_router), axis=-1)
    route_onehot = (
        routes[:, :, None] == jnp.arange(experts, dtype=jnp.int32)[None, None, :]
    ).astype(jnp.float32)
    picked = jnp.sum(route_onehot * router[:, None, :], axis=2)
    picked_total = jnp.sum(picked, axis=1, keepdims=True)
    gate_values = picked / picked_total
    flat_routes = routes.reshape(-1)
    flat_onehot = route_onehot.reshape(-1, experts).astype(jnp.int32)
    slot_ranks = jnp.sum((jnp.cumsum(flat_onehot, axis=0) - flat_onehot) * flat_onehot, axis=1)
    doubled = jnp.repeat(normed_two, 2, axis=0)
    outgoing = (
        jnp.zeros((experts, capacity, model_width), jnp.bfloat16)
        .at[flat_routes, slot_ranks]
        .set(doubled)
    )
    arrived = lax.all_to_all(
        outgoing.reshape(expert_count, local_experts * capacity, model_width),
        "expert",
        split_axis=0,
        concat_axis=0,
        tiled=True,
    )
    arrived = arrived.reshape(expert_count, local_experts, capacity, model_width)
    row_list = []
    pre_list = []
    act_list = []
    produced_list = []
    for slot_expert in range(local_experts):
        expert_rows = arrived[:, slot_expert].reshape(expert_count * capacity, model_width)
        pre_act = matmul(expert_rows, expert_first[slot_expert])
        activated = jax.nn.gelu(pre_act, approximate=False).astype(jnp.bfloat16)
        produced = matmul(activated, expert_second[slot_expert]).astype(jnp.bfloat16)
        row_list.append(expert_rows)
        pre_list.append(pre_act)
        act_list.append(activated)
        produced_list.append(produced.reshape(expert_count, 1, capacity, model_width))
    produced_all = jnp.concatenate(produced_list, axis=1).reshape(
        expert_count, local_experts * capacity, model_width
    )
    returned = lax.all_to_all(
        produced_all, "expert", split_axis=0, concat_axis=0, tiled=True
    ).reshape(experts, capacity, model_width)
    route_out = (
        returned[flat_routes, slot_ranks].reshape(rows_here, 2, model_width).astype(jnp.float32)
    )
    layer_out = hidden + jnp.sum(gate_values[:, :, None] * route_out, axis=1)
    grad_final = out_grad.astype(jnp.float32)
    grad_gates = jnp.sum(grad_final[:, None, :] * route_out, axis=2)
    grad_routes = (
        (gate_values[:, :, None] * grad_final[:, None, :])
        .astype(jnp.bfloat16)
        .reshape(-1, model_width)
    )
    grad_outgoing = (
        jnp.zeros((experts, capacity, model_width), jnp.bfloat16)
        .at[flat_routes, slot_ranks]
        .set(grad_routes)
    )
    grad_arrived = lax.all_to_all(
        grad_outgoing.reshape(expert_count, local_experts * capacity, model_width),
        "expert",
        split_axis=0,
        concat_axis=0,
        tiled=True,
    )
    grad_arrived = grad_arrived.reshape(expert_count, local_experts, capacity, model_width)
    grad_in_parts = []
    grad_out_parts = []
    back_list = []
    for slot_expert in range(local_experts):
        grad_rows = grad_arrived[:, slot_expert].reshape(expert_count * capacity, model_width)
        grad_act = contract_last(grad_rows, expert_second[slot_expert])
        grad_pre = (grad_act * gelu_slope(pre_list[slot_expert])).astype(jnp.bfloat16)
        grad_rows_in = contract_last(grad_pre, expert_first[slot_expert]).astype(jnp.bfloat16)
        back_list.append(grad_rows_in.reshape(expert_count, 1, capacity, model_width))
        grad_first = contract_first(row_list[slot_expert], grad_pre)
        grad_second = contract_first(act_list[slot_expert], grad_rows)
        grad_in_parts.append(grad_first)
        grad_out_parts.append(grad_second)
    grad_w_in, grad_w_out = (
        lax.psum_scatter(
            jnp.stack(grad_in_parts).astype(jnp.bfloat16), "shard", scatter_dimension=2, tiled=True
        ).astype(jnp.float32),
        lax.psum_scatter(
            jnp.stack(grad_out_parts).astype(jnp.bfloat16), "shard", scatter_dimension=1, tiled=True
        ).astype(jnp.float32),
    )
    back_all = jnp.concatenate(back_list, axis=1).reshape(
        expert_count, local_experts * capacity, model_width
    )
    sent_back = lax.all_to_all(back_all, "expert", split_axis=0, concat_axis=0, tiled=True).reshape(
        experts, capacity, model_width
    )
    grad_copies = (
        sent_back[flat_routes, slot_ranks].reshape(rows_here, 2, model_width).astype(jnp.float32)
    )
    weighted = jnp.sum(grad_gates * picked, axis=1, keepdims=True)
    grad_picked = grad_gates / picked_total - weighted / (picked_total * picked_total)
    grad_router = jnp.sum(grad_picked[:, :, None] * route_onehot, axis=1)
    grad_logits = (
        router * (grad_router - jnp.sum(router * grad_router, axis=1, keepdims=True))
    ).astype(jnp.bfloat16)
    grad_w_router = contract_first(normed_two, grad_logits)
    grad_normed_two = jnp.sum(grad_copies, axis=1) + contract_last(grad_logits, full_router)
    grad_norm_two, grad_gain_two = norm_back(hidden, inverse_two, gain_two, grad_normed_two)
    grad_hidden = grad_final + grad_norm_two
    grad_branch = grad_hidden.astype(jnp.bfloat16)
    grad_w_proj = contract_first(mixed_heads, grad_branch)
    grad_mixed = contract_last(grad_branch, full_proj).astype(jnp.bfloat16)
    row_dot = jnp.sum(
        grad_mixed.reshape(rows_here, head_count, head_width).astype(jnp.float32) * head_out, axis=2
    )
    all_log_norm, all_row_dot = (
        lax.all_gather(log_norm, "shard", axis=0, tiled=True),
        lax.all_gather(row_dot, "shard", axis=0, tiled=True),
    )
    key_heads = keys_here.reshape(rows_here, head_count, head_width)
    value_heads = values_here.reshape(rows_here, head_count, head_width)
    back_state = (
        jnp.zeros((rows_here, head_count, head_width), jnp.float32),
        jnp.zeros((rows_here, head_count, head_width), jnp.float32),
        jnp.zeros((seq_length, model_width), jnp.float32),
        jnp.zeros((bucket_count, head_count), jnp.float32),
    )
    piece_queries = lax.all_gather(queries, "shard", axis=0, tiled=True)
    piece_grads = lax.all_gather(grad_mixed, "shard", axis=0, tiled=True)
    piece_rows = piece_queries.shape[0]
    attend_block_rows = math.gcd(piece_rows, 512)

    def step(block_index, loop_state):
        grad_keys, grad_values, grad_queries, grad_bias = loop_state
        offset = block_index * attend_block_rows
        query_block = lax.dynamic_slice_in_dim(piece_queries, offset, attend_block_rows, 0).reshape(
            attend_block_rows, head_count, head_width
        )
        grad_block = lax.dynamic_slice_in_dim(piece_grads, offset, attend_block_rows, 0).reshape(
            attend_block_rows, head_count, head_width
        )
        query_pos = offset + jnp.arange(attend_block_rows, dtype=jnp.int32)
        query_seg = lax.dynamic_slice_in_dim(seq_segments, offset, attend_block_rows, 0)
        norm_block = lax.dynamic_slice_in_dim(all_log_norm, offset, attend_block_rows, 0)
        dot_block = lax.dynamic_slice_in_dim(all_row_dot, offset, attend_block_rows, 0)
        distance_bucket_table = bucket_block(query_pos, local_pos)
        bias_values = jnp.einsum(
            "yoc,yi->ioc",
            distance_bucket_table,
            position_bias_table,
            preferred_element_type=jnp.float32,
        )
        allowed = (
            (query_pos[:, None] >= local_pos[None, :]) & (query_seg[:, None] == local_seg[None, :])
        )[None]
        scores = (
            jnp.einsum("qhd,khd->hqk", query_block, key_heads, preferred_element_type=jnp.float32)
            * score_scale
            + bias_values
        )
        prob_block = jnp.where(allowed, jnp.exp(scores - norm_block.T[:, :, None]), 0.0)
        grad_values = grad_values + jnp.einsum(
            "hqk,qhd->khd",
            prob_block.astype(jnp.bfloat16),
            grad_block,
            preferred_element_type=jnp.float32,
        )
        grad_probs = jnp.einsum(
            "qhd,khd->hqk", grad_block, value_heads, preferred_element_type=jnp.float32
        )
        score_gradient = (prob_block * (grad_probs - dot_block.T[:, :, None])).astype(jnp.bfloat16)
        grad_keys = (
            grad_keys
            + jnp.einsum(
                "hqk,qhd->khd", score_gradient, query_block, preferred_element_type=jnp.float32
            )
            * score_scale
        )
        query_part = (
            jnp.einsum(
                "hqk,khd->qhd", score_gradient, key_heads, preferred_element_type=jnp.float32
            )
            * score_scale
        )
        grad_queries = lax.dynamic_update_slice_in_dim(
            grad_queries, query_part.reshape(attend_block_rows, model_width), offset, 0
        )
        grad_bias = grad_bias + jnp.einsum(
            "iof,mof->mi", score_gradient, distance_bucket_table, preferred_element_type=jnp.float32
        )
        return (grad_keys, grad_values, grad_queries, grad_bias)

    grad_keys, grad_values, grad_queries, grad_bias_table = lax.fori_loop(
        0, piece_rows // attend_block_rows, step, back_state
    )
    grad_query_here = lax.psum_scatter(
        grad_queries.astype(jnp.bfloat16), "shard", scatter_dimension=0, tiled=True
    )
    grad_key_here = grad_keys.reshape(rows_here, model_width).astype(jnp.bfloat16)
    grad_value_here = grad_values.reshape(rows_here, model_width).astype(jnp.bfloat16)
    grad_w_query = contract_first(normed_one, grad_query_here)
    grad_w_key = contract_first(normed_one, grad_key_here)
    grad_w_value = contract_first(normed_one, grad_value_here)
    grad_normed_one = (
        contract_last(grad_query_here, full_query)
        + contract_last(grad_key_here, full_key)
        + contract_last(grad_value_here, full_value)
    )
    grad_norm_one, grad_gain_one = norm_back(inputs, inverse_one, gain_one, grad_normed_one)
    tokens_grad = (grad_hidden + grad_norm_one).astype(jnp.bfloat16)
    shares = (
        lax.psum_scatter(
            grad_w_query.astype(jnp.bfloat16), "shard", scatter_dimension=0, tiled=True
        ).astype(jnp.float32),
        lax.psum_scatter(
            grad_w_key.astype(jnp.bfloat16), "shard", scatter_dimension=0, tiled=True
        ).astype(jnp.float32),
        lax.psum_scatter(
            grad_w_value.astype(jnp.bfloat16), "shard", scatter_dimension=0, tiled=True
        ).astype(jnp.float32),
        lax.psum_scatter(
            grad_w_proj.astype(jnp.bfloat16), "shard", scatter_dimension=0, tiled=True
        ).astype(jnp.float32),
        lax.psum_scatter(
            grad_w_router.astype(jnp.bfloat16), "shard", scatter_dimension=0, tiled=True
        ).astype(jnp.float32),
        lax.psum_scatter(
            grad_gain_one.astype(jnp.bfloat16), "shard", scatter_dimension=0, tiled=True
        ).astype(jnp.float32),
        lax.psum_scatter(
            grad_gain_two.astype(jnp.bfloat16), "shard", scatter_dimension=0, tiled=True
        ).astype(jnp.float32),
        lax.psum_scatter(
            grad_bias_table.astype(jnp.bfloat16), "shard", scatter_dimension=0, tiled=True
        ).astype(jnp.float32),
    )
    totals = (
        lax.psum(shares[0].astype(jnp.bfloat16), "expert").astype(jnp.float32),
        lax.psum(shares[1].astype(jnp.bfloat16), "expert").astype(jnp.float32),
        lax.psum(shares[2].astype(jnp.bfloat16), "expert").astype(jnp.float32),
        lax.psum(shares[3].astype(jnp.bfloat16), "expert").astype(jnp.float32),
        lax.psum(shares[4].astype(jnp.bfloat16), "expert").astype(jnp.float32),
        lax.psum(shares[5].astype(jnp.bfloat16), "expert").astype(jnp.float32),
        lax.psum(shares[6].astype(jnp.bfloat16), "expert").astype(jnp.float32),
        lax.psum(shares[7].astype(jnp.bfloat16), "expert").astype(jnp.float32),
    )
    return (
        layer_out.astype(jnp.bfloat16),
        tokens_grad,
        totals[0],
        totals[1],
        totals[2],
        totals[3],
        totals[4],
        totals[5],
        totals[6],
        totals[7],
        grad_w_in,
        grad_w_out,
    )


def solution(mesh):
    placed = (
        P(("expert", "shard"), None),
        P("shard", None),
        P("shard", None),
        P("shard", None),
        P("shard", None),
        P("shard", None),
        P("shard"),
        P("shard"),
        P("shard", None),
        P("expert", None, "shard"),
        P("expert", "shard", None),
        P(("expert", "shard"), None),
        P(("expert", "shard"), None),
        P("expert", None),
        P(),
    )
    return jax.shard_map(
        per_device,
        mesh=mesh,
        in_specs=placed,
        out_specs=(
            P(("expert", "shard"), None),
            P(("expert", "shard"), None),
            P("shard", None),
            P("shard", None),
            P("shard", None),
            P("shard", None),
            P("shard", None),
            P("shard"),
            P("shard"),
            P("shard", None),
            P("expert", None, "shard"),
            P("expert", "shard", None),
        ),
        check_vma=False,
    )
```

profile of v0, /device:TPU:0, one launch (start us, length us, event | category | flops | bytes accessed | tf_op | source)
XLA Modules:
  0.0 1376.5 jit_solution(1306899779285496502)
XLA Ops:
  13.2 13.6 all-reduce.8
  28.6 14.4 %all-gather.12.cloned.1.call-done = bf16[768,768]{1,0:T(8,128)(2,1)} async-done(((bf16[192,768]{1,0:T(8,128)(2,1)}), bf16[768,768]{1,0:T(8,128)(2,1)}) %all-gather.12.cloned.1.call-update) | async-done | bytes 1179664 | tf_op jit(solution)/shard_map/all_gather | solution.py:68
  45.7 28.4 %all-gather.18.cloned.1.call-done = bf16[768,768]{1,0:T(8,128)(2,1)} async-done(((bf16[192,768]{1,0:T(8,128)(2,1)}), bf16[768,768]{1,0:T(8,128)(2,1)}) %all-gather.18.cloned.1.call-update) | async-done | bytes 1179664 | tf_op jit(solution)/shard_map/all_gather | solution.py:69
  79.7 12.6 all_gather.52
  94.6 10.8 all-gather.16.cloned.1.call-done
  108.2 35.4 %all-gather.14.cloned.1.call-done = bf16[1024,768]{1,0:T(8,128)(2,1)} async-done(((bf16[256,768]{1,0:T(8,128)(2,1)}), bf16[1024,768]{1,0:T(8,128)(2,1)}) %all-gather.14.cloned.1.call-update) | async-done | bytes 1572880 | tf_op jit(solution)/shard_map/all_gather | solution.py:131
  143.6 38.0 %all-gather.20.cloned.1.call-done = bf16[1024,768]{1,0:T(8,128)(2,1)} async-done(((bf16[256,768]{1,0:T(8,128)(2,1)}), bf16[1024,768]{1,0:T(8,128)(2,1)}) %all-gather.20.cloned.1.call-update) | async-done | bytes 1572880 | tf_op jit(solution)/shard_map/all_gather | solution.py:132
  181.6 66.4 %while.38 = (s32[]{:T(128)}, f32[12,256]{1,0:T(8,128)S(1)}, f32[12,256]{1,0:T(8,128)S(1)}, f32[256,12,64]{0,2,1:T(8,128)S(1)}, s32[256]{0:T(256)S(1)}, /*index=5...) while((s32[]{:T(128)}, f32[12,256]{1,0:T(8,128)S(1)}, ...), condition=%wide.region_5.6_spmd.clone, body=%wide.region_2.5_spmd.clone.sunk | while | flops 532892416 | bytes 56706280 | solution.py:175
  188.0 9.2 copy.209
  221.1 9.5 copy.209
  254.1 69.2 %scatter_fusion = bf16[16,64,768]{2,1,0:T(8,128)(2,1)} fusion(bf16[16,64,768]{2,1,0:T(8,128)(2,1)} %broadcast.471.clone, s32[512]{0:T(512)S(1)} %bitcast.252, bf16[512,768]{1,0:T(8,128)(2,1)} %reshape.528), kind=kCustom, calls=%fused_computation.2 | custom fusion | bytes 2363392 | tf_op jit(solution)/shard_map/scatter | solution.py:198
  331.3 15.7 %all-gather = bf16[4,192,16]{1,2,0:T(8,128)(2,1)S(1)} all-gather(bf16[1,192,16]{1,2,0:T(8,128)(2,1)} %bitcast.289), channel_id=1, replica_groups=mesh['expert'=8,'shard'=4] {'shard'}, dimensions={0}, use_global_device_ids=true | all-gather | bytes 30720 | tf_op jit(solution)/shard_map/all_gather | solution.py:71
  354.0 69.4 %scatter_fusion.1 = bf16[16,64,768]{2,1,0:T(8,128)(2,1)} fusion(bf16[16,64,768]{2,1,0:T(8,128)(2,1)} %broadcast.471.clone.1, s32[512]{0:T(512)S(1)} %bitcast.253, bf16[512,768]{1,0:T(8,128)(2,1)} %multiply_convert_fusion.1), kind=kCustom, calls=%fused_computation.3 | custom fusion | bytes 2363392 | tf_op jit(solution)/shard_map/scatter | solution.py:241
  430.2 19.7 %all-to-all-done.2 = bf16[8,128,768]{2,1,0:T(8,128)(2,1)S(1)} async-done(((bf16[8,128,768]{2,1,0:T(8,128)(2,1)}), bf16[8,128,768]{2,1,0:T(8,128)(2,1)S(1)}, u32[]{:S(2)}, u32[]{:S(2)}) %all-to-all-start.2) | async-done | bytes 1572896 | tf_op jit(solution)/shard_map/all_to_all | solution.py:243
  450.1 18.8 %fusion.58 = (bf16[512,3072]{1,0:T(8,128)(2,1)}, f32[512,3072]{1,0:T(8,128)}) fusion(bf16[512,768]{1,0:T(8,128)(2,1)} %bitcast.280, bf16[2,768,3072]{2,1,0:T(8,128)(2,1)} %all-gather.24.cloned.1.call-done), kind=kOutput, calls=%fused_computation.83 | convolution fusion | flops 2518155264 | bytes 14942208 | tf_op jit(solution)/shard_map/dot_general | solution.py:13
  468.9 78.0 %all-gather.26.cloned.1.call-done = bf16[2,3072,768]{2,1,0:T(8,128)(2,1)} async-done(((bf16[2,768,768]{2,1,0:T(8,128)(2,1)}), bf16[2,3072,768]{2,1,0:T(8,128)(2,1)}) %all-gather.26.cloned.1.call-update) | async-done | bytes 9437200 | tf_op jit(solution)/shard_map/all_gather | solution.py:88
  556.5 17.4 %fusion.55 = (bf16[512,3072]{1,0:T(8,128)(2,1)}, f32[512,3072]{1,0:T(8,128)S(1)}) fusion(bf16[512,768]{1,0:T(8,128)(2,1)S(1)} %bitcast.278, bf16[2,768,3072]{2,1,0:T(8,128)(2,1)S(1)} %copy-done.63), kind=kOutput, calls=%fused_computation.80 | convolution fusion | flops 2518155264 | bytes 14942208 | tf_op jit(solution)/shard_map/dot_general | solution.py:13
  623.2 9.2 all-to-all-done.1
  665.4 13.7 all_gather.61
  680.4 13.5 all_gather.63
  698.8 103.9 %while.39 = (s32[]{:T(128)}, f32[256,12,64]{0,2,1:T(8,128)}, f32[256,12,64]{0,2,1:T(8,128)}, bf16[1024,768]{0,1:T(8,128)(2,1)}, f32[32,12]{0,1:T(8,128)}, /*inde...) while((s32[]{:T(128)}, f32[256,12,64]{0,2,1:T(8,128)}, ...), condition=%wide.region_25.26_spmd.clone, body=%wide.region_24.25_spmd.clone.sunk | while | flops 1248134656 | bytes 88122176 | solution.py:374
  707.3 9.1 copy.214
  758.9 9.1 copy.214
  810.7 26.6 %reduce-scatter.11.cloned.1.call-done = bf16[256,768]{0,1:T(8,128)(2,1)} async-done(((bf16[1024,768]{0,1:T(8,128)(2,1)}), bf16[256,768]{0,1:T(8,128)(2,1)}) %reduce-scatter.11.cloned.1.call-update) | async-done | bytes 393232 | tf_op jit(solution)/shard_map/reduce_scatter | solution.py:377
  847.4 20.3 %reduce-scatter.19.cloned.1.call-done = bf16[192,768]{1,0:T(8,128)(2,1)} async-done(((bf16[768,768]{1,0:T(8,128)(2,1)}), bf16[192,768]{1,0:T(8,128)(2,1)}) %reduce-scatter.19.cloned.1.call-update) | async-done | bytes 294928 | tf_op jit(solution)/shard_map/reduce_scatter | solution.py:402
  867.7 30.2 %reduce-scatter.15.cloned.1.call-done = bf16[192,768]{1,0:T(8,128)(2,1)} async-done(((bf16[768,768]{1,0:T(8,128)(2,1)}), bf16[192,768]{1,0:T(8,128)(2,1)}) %reduce-scatter.15.cloned.1.call-update) | async-done | bytes 294928 | tf_op jit(solution)/shard_map/reduce_scatter | solution.py:396
  897.9 30.1 %reduce-scatter.17.cloned.1.call-done = bf16[192,768]{1,0:T(8,128)(2,1)} async-done(((bf16[768,768]{1,0:T(8,128)(2,1)}), bf16[192,768]{1,0:T(8,128)(2,1)}) %reduce-scatter.17.cloned.1.call-update) | async-done | bytes 294928 | tf_op jit(solution)/shard_map/reduce_scatter | solution.py:399
  928.0 30.1 %reduce-scatter.13.cloned.1.call-done = bf16[192,768]{1,0:T(8,128)(2,1)} async-done(((bf16[768,768]{1,0:T(8,128)(2,1)}), bf16[192,768]{1,0:T(8,128)(2,1)}) %reduce-scatter.13.cloned.1.call-update) | async-done | bytes 294928 | tf_op jit(solution)/shard_map/reduce_scatter | solution.py:393
  1003.0 17.0 %all-reduce.7 = (bf16[768]{0:T(1024)(128)(2,1)S(1)}, bf16[768]{0:T(1024)(128)(2,1)S(1)}, bf16[32,12]{1,0:T(8,128)(2,1)S(1)}) all-reduce(bf16[768]{0:T(1024)(128)(2,1)S(1)} %get-tuple-element.798, bf16[768]{0:T(1024)(128)(2,1)} %get-tuple-element.794, bf16[32,12]{1,0:T(8,128)(2,1)} %copy.189), channel_id=8, replica_groups=mesh['expert'=8,'shard'=4] {'shard'}, use_global_device_ids=true, to_apply=%region_39.40.clone | all-reduce | flops 1920 | bytes 7680
  1020.2 22.6 %all-reduce.5 = (bf16[192,16]{0,1:T(8,128)(2,1)S(1)}, bf16[192]{0:T(256)(128)(2,1)S(1)}, bf16[192]{0:T(256)(128)(2,1)S(1)}, bf16[8,12]{1,0:T(8,128)(2,1)S(1)}) all-reduce(bf16[192,16]{0,1:T(8,128)(2,1)S(1)} %copy.192, bf16[192]{0:T(256)(128)(2,1)S(1)} %dynamic-slice.4, ...), channel_id=1, replica_groups=mesh['expert'=8,'shard'=4] {'expert'}, use_global_device_ids=true, to_apply=%region_37.38 | all-reduce | flops 3552 | bytes 14208 | tf_op jit(solution)/shard_map/psum | solution.py:423
  1054.0 146.9 %reduce-scatter.21.cloned.1.call-done = bf16[2,768,768]{2,1,0:T(8,128)(2,1)} async-done(((bf16[2,768,3072]{2,1,0:T(8,128)(2,1)}), bf16[2,768,768]{2,1,0:T(8,128)(2,1)}) %reduce-scatter.21.cloned.1.call-update) | async-done | bytes 2359312 | tf_op jit(solution)/shard_map/reduce_scatter | solution.py:265
  1205.2 160.3 %reduce-scatter.23.cloned.1.call-done = bf16[2,768,768]{2,1,0:T(8,128)(2,1)} async-done(((bf16[2,3072,768]{2,1,0:T(8,128)(2,1)}), bf16[2,768,768]{2,1,0:T(8,128)(2,1)}) %reduce-scatter.23.cloned.1.call-update) | async-done | bytes 2359312 | tf_op jit(solution)/shard_map/reduce_scatter | solution.py:268
  (411 shorter events, 359.3 us)
Async XLA Ops:
  7.2 98.3 %copy-start.5 = (bf16[256,768]{1,0:T(8,128)(2,1)S(1)}, bf16[256,768]{1,0:T(8,128)(2,1)}, u32[]{:S(2)}) copy-start(bf16[256,768]{1,0:T(8,128)(2,1)} %param.19) | copy-start | bytes 1179652
  7.2 86.6 %copy-start.44 = (s32[1,1024]{1,0:T(1,128)S(1)}, s32[1,1024]{1,0:T(1,128)}, u32[]{:S(2)}) copy-start(s32[1,1024]{1,0:T(1,128)} %param.32) | copy-start | bytes 12292
  7.2 35.7 %all-gather.12.cloned.1.call-start = ((), (), s32[]{:S(2)}) async-start(), calls=%async_computation.12 | async-start | bytes 1474560 | tf_op jit(solution)/shard_map/all_gather | solution.py:68
  8.0 66.2 %all-gather.18.cloned.1.call-start = ((), (), s32[]{:S(2)}) async-start(), calls=%async_computation.15 | async-start | bytes 1474560 | tf_op jit(solution)/shard_map/all_gather | solution.py:69
  8.7 96.7 %all-gather.16.cloned.1.call-start = ((), (), s32[]{:S(2)}) async-start(), calls=%async_computation.14 | async-start | bytes 1474560 | tf_op jit(solution)/shard_map/all_gather | solution.py:67
  9.5 134.1 %all-gather.14.cloned.1.call-start = ((), (), s32[]{:S(2)}) async-start(), calls=%async_computation.13 | async-start | bytes 1966080 | tf_op jit(solution)/shard_map/all_gather | solution.py:131
  26.8 80.4 %copy-start.40 = (f32[768]{0:T(1024)}, f32[768]{0:T(1024)S(1)}, u32[]{:S(2)}) copy-start(f32[768]{0:T(1024)S(1)} %convert_element_type.231) | copy-start | bytes 9220
  28.6 78.7 %copy-start.48 = (f32[256]{0:T(256)}, f32[256]{0:T(256)S(1)}, u32[]{:S(2)}) copy-start(f32[256]{0:T(256)S(1)} %get-tuple-element.894) | copy-start | bytes 3076
  45.6 135.9 %all-gather.20.cloned.1.call-start = ((), (), s32[]{:S(2)}) async-start(), calls=%async_computation.16 | async-start | bytes 1966080 | tf_op jit(solution)/shard_map/all_gather | solution.py:132
  76.8 171.4 %all-gather.22.cloned.1.call-start = ((), (), s32[]{:S(2)}) async-start(), calls=%async_computation.17 | async-start | bytes 1474560 | tf_op jit(solution)/shard_map/all_gather | solution.py:70
  77.4 372.7 %all-gather.24.cloned.1.call-start = ((), (), s32[]{:S(2)}) async-start(), calls=%async_computation.18 | async-start | bytes 11796480 | tf_op jit(solution)/shard_map/all_gather | solution.py:87
  78.1 468.8 %all-gather.26.cloned.1.call-start = ((), (), s32[]{:S(2)}) async-start(), calls=%async_computation.19 | async-start | bytes 11796480 | tf_op jit(solution)/shard_map/all_gather | solution.py:88
  248.0 75.3 %copy-start.2 = (f32[256,12,64]{0,2,1:T(8,128)}, f32[256,12,64]{0,2,1:T(8,128)S(1)}, u32[]{:S(2)}) copy-start(f32[256,12,64]{0,2,1:T(8,128)S(1)} %get-tuple-element.505) | copy-start | bytes 2359300
  248.0 75.3 %copy-start.19 = (f32[12,256]{1,0:T(8,128)}, f32[12,256]{1,0:T(8,128)S(1)}, u32[]{:S(2)}) copy-start(f32[12,256]{1,0:T(8,128)S(1)} %get-tuple-element.507) | copy-start | bytes 36868
  323.4 100.1 %all-to-all-start = ((bf16[8,128,768]{2,1,0:T(8,128)(2,1)}), bf16[8,128,768]{2,1,0:T(8,128)(2,1)S(1)}, u32[]{:S(2)}, u32[]{:S(2)}) async-start(bf16[8,128,768]{2,1,0:T(8,128)(2,1)} %bitcast.10), calls=%async_computation | async-start | bytes 3145728 | tf_op jit(solution)/shard_map/all_to_all | solution.py:200
  423.4 26.5 %all-to-all-start.2 = ((bf16[8,128,768]{2,1,0:T(8,128)(2,1)}), bf16[8,128,768]{2,1,0:T(8,128)(2,1)S(1)}, u32[]{:S(2)}, u32[]{:S(2)}) async-start(bf16[8,128,768]{2,1,0:T(8,128)(2,1)} %bitcast.25), calls=%async_computation.2 | async-start | bytes 3145728 | tf_op jit(solution)/shard_map/all_to_all | solution.py:243
  450.0 96.9 %copy-start.34 = (bf16[8,1,64,768]{3,2,1,0:T(8,128)(2,1)}, bf16[8,1,64,768]{3,2,1,0:T(8,128)(2,1)S(1)}, u32[]{:S(2)}) copy-start(bf16[8,1,64,768]{3,2,1,0:T(8,128)(2,1)S(1)} %get-tuple-element.888) | copy-start | bytes 2359300
  450.0 123.9 %copy-start.32 = (bf16[8,1,64,768]{3,2,1,0:T(8,128)(2,1)}, bf16[8,1,64,768]{3,2,1,0:T(8,128)(2,1)S(1)}, u32[]{:S(2)}) copy-start(bf16[8,1,64,768]{3,2,1,0:T(8,128)(2,1)S(1)} %get-tuple-element.887) | copy-start | bytes 2359300
  583.2 24.7 %all-to-all-start.3 = ((bf16[8,128,768]{2,1,0:T(8,128)(2,1)}), bf16[8,128,768]{2,1,0:T(8,128)(2,1)S(1)}, u32[]{:S(2)}, u32[]{:S(2)}) async-start(bf16[8,128,768]{2,1,0:T(8,128)(2,1)} %bitcast.33), calls=%async_computation.3 | async-start | bytes 3145728 | tf_op jit(solution)/shard_map/all_to_all | solution.py:275
  607.8 24.5 %all-to-all-start.1 = ((bf16[8,128,768]{2,1,0:T(8,128)(2,1)}), bf16[8,128,768]{2,1,0:T(8,128)(2,1)S(1)}, u32[]{:S(2)}, u32[]{:S(2)}) async-start(bf16[8,128,768]{2,1,0:T(8,128)(2,1)} %bitcast.263), calls=%async_computation.1 | async-start | bytes 3145728 | tf_op jit(solution)/shard_map/all_to_all | solution.py:224
  611.4 82.5 %all-gather.28.cloned.1.call-start = ((), (), s32[]{:S(2)}) async-start(), calls=%async_computation.20 | async-start | bytes 1966080 | tf_op jit(solution)/shard_map/all_gather | solution.py:309
  612.5 84.9 %all-gather.30.cloned.1.call-start = ((), (), s32[]{:S(2)}) async-start(), calls=%async_computation.21 | async-start | bytes 1966080 | tf_op jit(solution)/shard_map/all_gather | solution.py:310
  662.2 175.1 %reduce-scatter.11.cloned.1.call-start = ((), (), s32[]{:S(2)}) async-start(), calls=%async_computation.22 | async-start | bytes 1966080 | tf_op jit(solution)/shard_map/reduce_scatter | solution.py:377
  802.9 64.8 %reduce-scatter.19.cloned.1.call-start = ((), (), s32[]{:S(2)}) async-start(), calls=%async_computation.26 | async-start | bytes 1474560 | tf_op jit(solution)/shard_map/reduce_scatter | solution.py:402
  805.8 92.1 %reduce-scatter.15.cloned.1.call-start = ((), (), s32[]{:S(2)}) async-start(), calls=%async_computation.24 | async-start | bytes 1474560 | tf_op jit(solution)/shard_map/reduce_scatter | solution.py:396
  808.8 119.2 %reduce-scatter.17.cloned.1.call-start = ((), (), s32[]{:S(2)}) async-start(), calls=%async_computation.25 | async-start | bytes 1474560 | tf_op jit(solution)/shard_map/reduce_scatter | solution.py:399
  810.6 147.5 %reduce-scatter.13.cloned.1.call-start = ((), (), s32[]{:S(2)}) async-start(), calls=%async_computation.23 | async-start | bytes 1474560 | tf_op jit(solution)/shard_map/reduce_scatter | solution.py:393
  840.0 155.2 %reduce-scatter.25.cloned.1.call-start = ((), (), s32[]{:S(2)}) async-start(), calls=%async_computation.29 | async-start | bytes 245760
  841.1 117.1 %copy-start.37 = (bf16[8,1,64,768]{3,2,1,0:T(8,128)(2,1)S(1)}, bf16[8,1,64,768]{3,2,1,0:T(8,128)(2,1)}, u32[]{:S(2)}) copy-start(bf16[8,1,64,768]{3,2,1,0:T(8,128)(2,1)} %get-tuple-element.889) | copy-start | bytes 2359300
  841.1 205.7 %all-reduce.11.cloned.1.call-start = ((), (), s32[]{:S(2)}) async-start(), calls=%async_computation.30 | async-start | bytes 2359296 | tf_op jit(solution)/shard_map/psum | solution.py:419
  958.1 242.8 %reduce-scatter.21.cloned.1.call-start = ((), (), s32[]{:S(2)}) async-start(), calls=%async_computation.27 | async-start | bytes 11796480 | tf_op jit(solution)/shard_map/reduce_scatter | solution.py:265
  972.7 392.8 %reduce-scatter.23.cloned.1.call-start = ((), (), s32[]{:S(2)}) async-start(), calls=%async_computation.28 | async-start | bytes 11796480 | tf_op jit(solution)/shard_map/reduce_scatter | solution.py:268
  (74 other events, 1900.4 us)
Sparse Core Ops, SparseCore 0:
  9.6 33.2 all-gather.11
  44.5 29.5 all-gather.17
  75.7 29.7 all-gather.15
  107.4 36.1 all-gather.13
  145.6 35.9 all-gather.19
  183.0 29.2 all-gather.21
  213.9 166.3 all-gather.23
  381.9 164.9 all-gather.25
  614.4 35.7 all-gather.27
  662.3 35.0 all-gather.29
  803.0 34.2 reduce-scatter.10
  839.5 28.1 reduce-scatter.18
  870.0 27.8 reduce-scatter.14
  900.1 27.8 reduce-scatter.16
  930.2 27.8 reduce-scatter.12
  960.8 18.0 reduce-scatter.24
  982.5 55.7 all-reduce.10
  1040.5 160.4 reduce-scatter.20
  1203.3 162.1 reduce-scatter.22
where the time goes:
time: 1390 us; the launch traced here: 1380 us
  waiting for transfers between devices  695 us (50%)
  local copies, waits for them, and re-layouts  251 us (18%)
  matrix products  215 us (15%)
  blocking collectives  109 us (8%)
  other arithmetic  71.7 us (5%)
  starting transfers between devices  17.4 us (1%)
  between operations  17.4 us (1%)
    reduce_scatter x1, waiting for transfers between devices, per_device(): lax.psum_scatter(jnp.stack(grad_out_parts).astype(jnp.bfloat16), 'shard',...  160 us
    reduce_scatter x1, waiting for transfers between devices, per_device(): lax.psum_scatter(jnp.stack(grad_in_parts).astype(jnp.bfloat16), 'shard',...  147 us
    all_gather x1, waiting for transfers between devices, per_device(): lax.all_gather(w_out, 'shard', axis=1, tiled=True)  78 us
    scatter x1, local copies, waits for them, and re-layouts, per_device(): grad_outgoing = jnp.zeros((experts, capacity, model_width), jnp.bfloat16)...  69.4 us
    scatter x1, local copies, waits for them, and re-layouts, per_device(): outgoing = jnp.zeros((experts, capacity, model_width), jnp.bfloat16).at[f...  69.2 us
    dot_general x9, matrix products, matmul(): return jnp.dot(left_operand, right_side, preferred_element_type=jnp.float32)  57.6 us
    all_gather x1, waiting for transfers between devices, per_device(): piece_values = lax.all_gather(values_here, 'shard', axis=0, tiled=True)  38 us
    dot_general x4, local copies, waits for them, and re-layouts, step(): jnp.einsum('yoc,yi->ioc', distance_bucket_table, position_bias_table, pre...  37 us
  transfers between devices with their start and end apart: 23, of which 17 were waited for; matrix products, arithmetic and copies ran while one was open for 28% of the time, Pallas kernels for 0%

commit v1 on v0

--- a/solution.py
+++ b/solution.py
@@ -3,6 +3,8 @@
 import jax
 import jax.numpy as jnp
 from jax import lax
+from jax.experimental import pallas as pl
+from jax.experimental.pallas import tpu as pltpu
 from jax.sharding import PartitionSpec as P
 
 EPSILON = 1e-06
@@ -46,7 +48,7 @@
     return (grad_values, grad_gain)
 
 
-def per_device(
+def routed_plan(
     tokens,
     w_query,
     w_key,
@@ -441,6 +443,463 @@
     )
 
 
+VMEM_BYTES = 60 * 1024 * 1024
+TILE = 256
+PACK_ROWS = 16
+DENSE_TOKENS = 16384
+
+
+def attend_forward(qkv_ref, skew_ref, seg_col_ref, seg_row_ref, out_ref, prob_ref, toeplitz):
+    heads, seq_length = prob_ref.shape[0], prob_ref.shape[1]
+    width = out_ref.shape[1] // heads
+    tiles = seq_length // TILE
+    scale = width ** (-0.5)
+    lower = lax.broadcasted_iota(jnp.int32, (TILE, TILE), 0) >= lax.broadcasted_iota(
+        jnp.int32, (TILE, TILE), 1
+    )
+    for head in range(heads):
+        for delta in range(tiles):
+            row = skew_ref[head, delta : delta + 1, :]
+            wide = jnp.broadcast_to(row, (TILE, 2 * TILE))
+            turned = pltpu.roll(wide, 0, 1, stride=1, stride_axis=0)[:, :TILE]
+            if delta == 0:
+                turned = jnp.where(lower, turned, NEG_BIG)
+            toeplitz[delta] = turned
+        query_cols = pl.ds(head * width, width)
+        key_cols = pl.ds((heads + head) * width, width)
+        value_cols = pl.ds((2 * heads + head) * width, width)
+        for tile in range(tiles):
+            rows = pl.ds(tile * TILE, TILE)
+            extent = (tile + 1) * TILE
+            query = qkv_ref[rows, query_cols]
+            scores = contract_last(query, qkv_ref[pl.ds(0, extent), key_cols]) * scale
+            bias = jnp.concatenate([toeplitz[tile - other] for other in range(tile + 1)], axis=1)
+            same = seg_col_ref[rows, :] == seg_row_ref[:, pl.ds(0, extent)]
+            scores = jnp.where(same, scores + bias, NEG_BIG)
+            top = jnp.max(scores, axis=1, keepdims=True)
+            weight = jnp.exp(scores - top)
+            total = jnp.sum(weight, axis=1, keepdims=True)
+            prob = (weight * (1.0 / total)).astype(jnp.bfloat16)
+            prob_ref[head, rows, pl.ds(0, extent)] = prob
+            out_ref[rows, query_cols] = matmul(
+                prob, qkv_ref[pl.ds(0, extent), value_cols]
+            ).astype(jnp.bfloat16)
+
+
+def attend_backward(qkv_ref, grad_ref, prob_ref, grad_qkv_ref, diag_ref, keys_acc, values_acc, blocks):
+    heads, seq_length = prob_ref.shape[0], prob_ref.shape[1]
+    width = grad_ref.shape[1] // heads
+    tiles = seq_length // TILE
+    scale = width ** (-0.5)
+    flip = (
+        lax.broadcasted_iota(jnp.int32, (TILE, TILE), 0)
+        + lax.broadcasted_iota(jnp.int32, (TILE, TILE), 1)
+        == TILE - 1
+    ).astype(jnp.float32)
+    for head in range(heads):
+        query_cols = pl.ds(head * width, width)
+        key_cols = pl.ds((heads + head) * width, width)
+        value_cols = pl.ds((2 * heads + head) * width, width)
+        keys_acc[...] = jnp.zeros_like(keys_acc)
+        values_acc[...] = jnp.zeros_like(values_acc)
+        blocks[...] = jnp.zeros_like(blocks)
+        for tile in range(tiles):
+            rows = pl.ds(tile * TILE, TILE)
+            extent = (tile + 1) * TILE
+            seen = pl.ds(0, extent)
+            query = qkv_ref[rows, query_cols]
+            grad = grad_ref[rows, query_cols]
+            prob = prob_ref[head, rows, seen]
+            wide = prob.astype(jnp.float32)
+            grad_prob = contract_last(grad, qkv_ref[seen, value_cols])
+            dots = jnp.sum(wide * grad_prob, axis=1, keepdims=True)
+            grad_score = (wide * (grad_prob - dots)).astype(jnp.bfloat16)
+            grad_qkv_ref[rows, query_cols] = (
+                matmul(grad_score, qkv_ref[seen, key_cols]) * scale
+            ).astype(jnp.bfloat16)
+            keys_acc[seen, :] += contract_first(grad_score, query)
+            values_acc[seen, :] += contract_first(prob, grad)
+            for other in range(tile + 1):
+                blocks[tile - other] += grad_score[:, other * TILE : (other + 1) * TILE].astype(
+                    jnp.float32
+                )
+        grad_qkv_ref[:, key_cols] = (keys_acc[...] * scale).astype(jnp.bfloat16)
+        grad_qkv_ref[:, value_cols] = values_acc[...].astype(jnp.bfloat16)
+        for delta in range(tiles):
+            flipped = jnp.dot(
+                flip,
+                blocks[delta],
+                precision=lax.Precision.HIGHEST,
+                preferred_element_type=jnp.float32,
+            )
+            padded = jnp.concatenate([flipped, jnp.zeros_like(flipped)], axis=1)
+            turned = pltpu.roll(padded, 0, 1, stride=1, stride_axis=0)
+            diag_ref[head, delta : delta + 1, :] = jnp.sum(turned, axis=0, keepdims=True)
+
+
+def expert_step(
+    ranks_ref,
+    gates_ref,
+    rows_ref,
+    grads_ref,
+    first_ref,
+    second_ref,
+    out_ref,
+    back_ref,
+    dots_ref,
+    grad_first_ref,
+    grad_second_ref,
+):
+    local_experts, group, _, block = ranks_ref.shape
+    capacity = 64 * block // 256
+
+    @pl.when(pl.program_id(0) == 0)
+    def _():
+        grad_first_ref[...] = jnp.zeros_like(grad_first_ref)
+        grad_second_ref[...] = jnp.zeros_like(grad_second_ref)
+
+    slot = lax.broadcasted_iota(jnp.int32, (capacity, block), 0).astype(jnp.float32)
+    for expert in range(local_experts):
+        picks = [ranks_ref[expert, at] == slot for at in range(group)]
+        ones = [pick.astype(jnp.float32).astype(jnp.bfloat16) for pick in picks]
+        gate = jnp.concatenate(
+            [
+                jnp.sum(jnp.where(picks[at], gates_ref[expert, at], 0.0), axis=1, keepdims=True)
+                for at in range(group)
+            ],
+            axis=0,
+        )
+        rows = jnp.concatenate(
+            [matmul(ones[at], rows_ref[at]).astype(jnp.bfloat16) for at in range(group)], axis=0
+        )
+        grads = jnp.concatenate(
+            [matmul(ones[at], grads_ref[at, pl.ds(0, block), :]) for at in range(group)], axis=0
+        )
+        pre = matmul(rows, first_ref[expert])
+        half = 0.5 * (1.0 + lax.erf(pre * 0.7071067811865476))
+        act = (pre * half).astype(jnp.bfloat16)
+        slope = half + pre * jnp.exp(-0.5 * pre * pre) * 0.3989422804014327
+        produced = matmul(act, second_ref[expert])
+        dots = jnp.sum(grads * produced, axis=1, keepdims=True)
+        given = (gate * grads).astype(jnp.bfloat16)
+        weighted = (gate * produced).astype(jnp.bfloat16)
+        grad_pre = (contract_last(given, second_ref[expert]) * slope).astype(jnp.bfloat16)
+        back = contract_last(grad_pre, first_ref[expert]).astype(jnp.bfloat16)
+        grad_first_ref[expert] += contract_first(rows, grad_pre)
+        grad_second_ref[expert] += contract_first(act, given)
+        for at in range(group):
+            part = slice(at * capacity, (at + 1) * capacity)
+            out_part = contract_first(ones[at], weighted[part])
+            back_part = contract_first(ones[at], back[part])
+            if expert > 0:
+                out_part = out_part + out_ref[at].astype(jnp.float32)
+                back_part = back_part + back_ref[at].astype(jnp.float32)
+            out_ref[at] = out_part.astype(jnp.bfloat16)
+            back_ref[at] = back_part.astype(jnp.bfloat16)
+            dots_ref[expert, at] = jnp.sum(
+                jnp.where(picks[at], dots[part], 0.0), axis=0, keepdims=True
+            )
+
+
+def run_experts(ranks, gates, rows, grads, first, second):
+    local_experts, blocks, _, block = ranks.shape
+    width = rows.shape[2]
+    group = math.gcd(blocks, 4)
+    small = pl.BlockSpec((local_experts, group, 1, block), lambda i: (0, i, 0, 0))
+    fixed = lambda shape: pl.BlockSpec(
+        shape, lambda i: (0, 0, 0), pipeline_mode=pl.Buffered(1)
+    )
+    tall = pl.BlockSpec((group, block, width), lambda i: (i, 0, 0))
+    return pl.pallas_call(
+        expert_step,
+        grid=(blocks // group,),
+        in_specs=[
+            small,
+            small,
+            tall,
+            pl.BlockSpec((group, grads.shape[1], width), lambda i: (i, 0, 0)),
+            fixed(first.shape),
+            fixed(second.shape),
+        ],
+        out_specs=[tall, tall, small, fixed(first.shape), fixed(second.shape)],
+        out_shape=[
+            jax.ShapeDtypeStruct((blocks, block, width), jnp.bfloat16),
+            jax.ShapeDtypeStruct((blocks, block, width), jnp.bfloat16),
+            jax.ShapeDtypeStruct(ranks.shape, jnp.float32),
+            jax.ShapeDtypeStruct(first.shape, jnp.float32),
+            jax.ShapeDtypeStruct(second.shape, jnp.float32),
+        ],
+        compiler_params=pltpu.CompilerParams(vmem_limit_bytes=VMEM_BYTES),
+    )(ranks, gates, rows, grads, first, second)
+
+
+def pad_rows(flat, rows, width):
+    return jnp.concatenate(
+        [flat, jnp.zeros((rows * width - flat.shape[0],), flat.dtype)]
+    ).reshape(rows, width)
+
+
+def dense_plan(
+    tokens,
+    w_query,
+    w_key,
+    w_value,
+    w_out_attn,
+    w_router,
+    gain_attn,
+    gain_moe,
+    rel_bias,
+    w_in,
+    w_out,
+    out_grad,
+    routes,
+    segments,
+    buckets,
+):
+    block, width = tokens.shape
+    shards = lax.axis_size("shard")
+    groups = lax.axis_size("expert")
+    seq_length = block * shards
+    head_count = rel_bias.shape[1]
+    heads = head_count // shards
+    head_width = width // head_count
+    owned = heads * head_width
+    experts = w_router.shape[1]
+    local_experts = w_in.shape[0]
+    bucket_count = rel_bias.shape[0] * shards
+    part_rows = w_router.shape[0]
+    blocks = groups * shards
+    tiles = seq_length // TILE
+    shard_at = lax.axis_index("shard")
+    expert_at = lax.axis_index("expert")
+    bf16, f32 = jnp.bfloat16, jnp.float32
+
+    small = jnp.concatenate(
+        [w_router.reshape(-1), gain_attn.reshape(-1), gain_moe.reshape(-1), rel_bias.reshape(-1)]
+    )
+    opening = jnp.concatenate([tokens, pad_rows(small, PACK_ROWS, width)], axis=0)
+    opened = lax.all_gather(opening, "shard", axis=0)
+    tokens_seq = opened[:, :block].reshape(seq_length, width)
+    smalls = opened[:, block:].reshape(shards, -1)
+    at = part_rows * experts
+    full_router = smalls[:, :at].reshape(width, experts)
+    gain_one = smalls[:, at : at + part_rows].reshape(width).astype(f32)
+    gain_two = smalls[:, at + part_rows : at + 2 * part_rows].reshape(width).astype(f32)
+    at = at + 2 * part_rows
+    table = smalls[:, at : at + rel_bias.size].reshape(bucket_count, head_count)
+
+    stacked = jnp.stack([w_query, w_key, w_value], axis=1).reshape(part_rows, 3, shards, owned)
+    stacked = stacked.transpose(2, 0, 1, 3).reshape(shards, part_rows, 3 * owned)
+    own_qkv = lax.all_to_all(stacked, "shard", split_axis=0, concat_axis=0, tiled=True)
+    own_qkv = own_qkv.reshape(width, 3 * owned)
+    full_proj = lax.all_gather(w_out_attn, "shard", axis=0, tiled=True)
+
+    closing = jnp.concatenate(
+        [out_grad, pad_rows(routes.T.reshape(-1).astype(bf16), PACK_ROWS, width)], axis=0
+    )
+    closed = lax.all_gather(closing, ("expert", "shard"), axis=0)
+
+    inputs_seq = tokens_seq.astype(f32)
+    normed_seq, inverse_seq = norm_parts(inputs_seq, gain_one)
+    normed_seq = normed_seq.astype(bf16)
+    qkv = matmul(normed_seq, own_qkv).astype(bf16)
+    bucket_hot = (buckets[:, None] == jnp.arange(bucket_count, dtype=jnp.int32)[None, :]).astype(bf16)
+    own_table = lax.dynamic_slice_in_dim(table, shard_at * heads, heads, 1)
+    by_distance = lax.dot_general(
+        own_table, bucket_hot, (((0,), (1,)), ((), ())), preferred_element_type=f32
+    )
+    descending = jnp.pad(by_distance, ((0, 0), (TILE, TILE)))[:, ::-1]
+    pieces = []
+    for delta in range(tiles):
+        low_at = seq_length + TILE - 1 - delta * TILE
+        pieces.append(
+            jnp.concatenate(
+                [descending[:, low_at : low_at + TILE], descending[:, low_at - TILE : low_at]], axis=1
+            )
+        )
+    skew = jnp.stack(pieces, axis=1)
+    seg = segments[0]
+    mixed, prob = pl.pallas_call(
+        attend_forward,
+        out_shape=[
+            jax.ShapeDtypeStruct((seq_length, owned), bf16),
+            jax.ShapeDtypeStruct((heads, seq_length, seq_length), bf16),
+        ],
+        scratch_shapes=[pltpu.VMEM((tiles, TILE, TILE), f32)],
+        compiler_params=pltpu.CompilerParams(vmem_limit_bytes=VMEM_BYTES),
+    )(qkv, skew, seg[:, None], seg[None, :])
+    mixed_here = lax.all_to_all(
+        mixed.reshape(shards, block, owned), "shard", split_axis=0, concat_axis=0, tiled=True
+    )
+    mixed_here = mixed_here.transpose(1, 0, 2).reshape(block, width)
+
+    inputs = tokens.astype(f32)
+    hidden = inputs + matmul(mixed_here, full_proj)
+    normed_two, inverse_two = norm_parts(hidden, gain_two)
+    normed_two = normed_two.astype(bf16)
+    normed_all = lax.all_gather(normed_two, ("expert", "shard"), axis=0)
+    expert_ids = jnp.arange(experts, dtype=jnp.int32)
+
+    grads_all = closed
+    routes_all = closed[:, block].reshape(blocks, width)[:, : 2 * block]
+    routes_all = routes_all.reshape(blocks, 2, block).astype(jnp.int32)
+    logits_all = lax.dot_general(
+        full_router, normed_all, (((0,), (2,)), ((), ())), preferred_element_type=f32
+    )
+    router_all = jax.nn.softmax(logits_all, axis=0)
+    own_ids = expert_at * local_experts + jnp.arange(local_experts, dtype=jnp.int32)
+    named = (routes_all[None] == own_ids[:, None, None, None]).any(axis=2)
+    first_hot = routes_all[None, :, 0] == expert_ids[:, None, None]
+    second_hot = routes_all[None, :, 1] == expert_ids[:, None, None]
+    picked_sum = jnp.sum(jnp.where(first_hot | second_hot, router_all, 0.0), axis=0)
+    own_router = lax.dynamic_slice_in_dim(router_all, expert_at * local_experts, local_experts, 0)
+    gates_all = jnp.where(named, own_router / picked_sum[None], 0.0)
+    before = (jnp.arange(block)[:, None] < jnp.arange(block)[None, :]).astype(bf16)
+    ranks = matmul(named.astype(bf16).reshape(-1, block), before).reshape(named.shape)
+    ranks = jnp.where(named, ranks, -1.0)
+    out_parts, back_parts, dots, grad_w_in, grad_w_out = run_experts(
+        ranks[:, :, None, :], gates_all[:, :, None, :], normed_all, grads_all, w_in, w_out
+    )
+    dots = dots[:, :, 0, :]
+    dots_by_choice = jnp.sum(
+        jnp.where(routes_all[None] == own_ids[:, None, None, None], dots[:, :, None, :], 0.0), axis=0
+    )
+    dots_rows = jnp.pad(
+        dots_by_choice.astype(bf16).reshape(blocks, 1, 2 * block),
+        ((0, 0), (0, PACK_ROWS - 1), (0, width - 2 * block)),
+    )
+    back_parts = jnp.concatenate([back_parts, dots_rows], axis=1)
+    back_here = lax.psum_scatter(back_parts, ("expert", "shard"), scatter_dimension=0, tiled=True)[0]
+    out_here = lax.psum_scatter(out_parts, ("expert", "shard"), scatter_dimension=0, tiled=True)[0]
+    layer_out = (hidden + out_here.astype(f32)).astype(bf16)
+
+    router = jax.nn.softmax(matmul(normed_two, full_router), axis=-1)
+    route_onehot = (routes[:, :, None] == expert_ids[None, None, :]).astype(f32)
+    picked = jnp.sum(route_onehot * router[:, None, :], axis=2)
+    picked_total = jnp.sum(picked, axis=1, keepdims=True)
+    grad_gates = back_here[block, : 2 * block].reshape(2, block).T.astype(f32)
+    weighted = jnp.sum(grad_gates * picked, axis=1, keepdims=True)
+    grad_picked = grad_gates / picked_total - weighted / (picked_total * picked_total)
+    grad_router = jnp.sum(grad_picked[:, :, None] * route_onehot, axis=1)
+    grad_logits = (
+        router * (grad_router - jnp.sum(router * grad_router, axis=1, keepdims=True))
+    ).astype(bf16)
+    grad_w_router = contract_first(normed_two, grad_logits)
+    grad_normed_two = back_here[:block].astype(f32) + contract_last(grad_logits, full_router)
+    grad_norm_two, grad_gain_two = norm_back(hidden, inverse_two, gain_two, grad_normed_two)
+    grad_hidden = out_grad.astype(f32) + grad_norm_two
+    grad_branch = lax.all_gather(grad_hidden.astype(bf16), "shard", axis=0, tiled=True)
+
+    grad_w_proj = contract_first(mixed, grad_branch)
+    grad_mixed = contract_last(grad_branch, w_out_attn).astype(bf16)
+    grad_qkv, diagonals = pl.pallas_call(
+        attend_backward,
+        out_shape=[
+            jax.ShapeDtypeStruct((seq_length, 3 * owned), bf16),
+            jax.ShapeDtypeStruct((heads, tiles, 2 * TILE), f32),
+        ],
+        scratch_shapes=[
+            pltpu.VMEM((seq_length, head_width), f32),
+            pltpu.VMEM((seq_length, head_width), f32),
+            pltpu.VMEM((tiles, TILE, TILE), f32),
+        ],
+        compiler_params=pltpu.CompilerParams(vmem_limit_bytes=VMEM_BYTES),
+    )(qkv, grad_mixed, prob)
+    grad_normed_one = contract_last(grad_qkv, own_qkv)
+    norm_one_here = lax.psum_scatter(
+        grad_normed_one.astype(bf16), "shard", scatter_dimension=0, tiled=True
+    ).astype(f32)
+    grad_gain_one = jnp.sum(grad_normed_one * inputs_seq * inverse_seq, axis=0)
+    by_distance_grad = jnp.zeros((heads, seq_length + TILE), f32)
+    for delta in range(tiles):
+        piece = diagonals[:, delta, ::-1]
+        start = delta * TILE
+        by_distance_grad = by_distance_grad.at[:, start : start + 2 * TILE].add(piece)
+    by_distance_grad = by_distance_grad[:, TILE : TILE + seq_length]
+    grad_table = lax.dot_general(
+        bucket_hot.astype(f32),
+        by_distance_grad,
+        (((0,), (1,)), ((), ())),
+        precision=lax.Precision.HIGHEST,
+        preferred_element_type=f32,
+    )
+    grad_qkv_full = contract_first(normed_seq, grad_qkv)
+
+    bias_rows = grad_table.reshape(shards, -1)
+    tail = jnp.concatenate(
+        [
+            grad_w_router.reshape(shards, -1),
+            grad_gain_one.reshape(shards, -1),
+            grad_gain_two.reshape(shards, -1),
+            bias_rows,
+        ],
+        axis=1,
+    )
+    tail_rows = -(-tail.shape[1] // (3 * owned))
+    tail_rows = -(-tail_rows // 16) * 16
+    tail = jnp.pad(tail, ((0, 0), (0, tail_rows * 3 * owned - tail.shape[1])))
+    leaving = jnp.concatenate(
+        [
+            grad_qkv_full.reshape(shards, part_rows, 3 * owned),
+            tail.reshape(shards, tail_rows, 3 * owned),
+        ],
+        axis=1,
+    ).astype(bf16)
+    landed = lax.all_to_all(leaving, "shard", split_axis=0, concat_axis=0, tiled=True)
+    landed_tail = landed[:, part_rows:].reshape(shards, -1)
+    plain = part_rows * (experts + 2)
+    summed_tail = jnp.sum(landed_tail[:, :plain].astype(f32), axis=0).astype(bf16)
+    bias_count = rel_bias.shape[0] * heads
+    final = jnp.concatenate(
+        [
+            landed[:, :part_rows].reshape(-1),
+            grad_w_proj.astype(bf16).reshape(-1),
+            summed_tail,
+            landed_tail[:, plain : plain + bias_count].reshape(-1),
+        ]
+    )
+    length = final.shape[0]
+    final = jnp.pad(final, (0, -length % 2048)).reshape(-1, 128)
+    final = lax.psum(final, "expert").reshape(-1).astype(f32)
+    size = part_rows * width
+    grads_qkv = final[: 3 * size].reshape(shards, part_rows, 3, owned)
+    grads_qkv = grads_qkv.transpose(2, 1, 0, 3).reshape(3, part_rows, width)
+    proj_total = final[3 * size : 4 * size].reshape(part_rows, width)
+    rest = final[4 * size : length]
+    router_total = rest[: part_rows * experts].reshape(part_rows, experts)
+    gain_one_total = rest[part_rows * experts : part_rows * (experts + 1)]
+    gain_two_total = rest[part_rows * (experts + 1) : plain]
+    bias_total = rest[plain:].reshape(shards, rel_bias.shape[0], heads)
+    bias_total = bias_total.transpose(1, 0, 2).reshape(rel_bias.shape)
+
+    inverse_one = lax.rsqrt(jnp.mean(inputs * inputs, axis=-1, keepdims=True) + EPSILON)
+    grad_norm_one, _ = norm_back(inputs, inverse_one, gain_one, norm_one_here)
+    tokens_grad = (grad_hidden + grad_norm_one).astype(bf16)
+    return (
+        layer_out,
+        tokens_grad,
+        grads_qkv[0],
+        grads_qkv[1],
+        grads_qkv[2],
+        proj_total,
+        router_total,
+        gain_one_total,
+        gain_two_total,
+        bias_total,
+        grad_w_in,
+        grad_w_out,
+    )
+
+
+def per_device(*arguments):
+    tokens, rel_bias = arguments[0], arguments[8]
+    shards = lax.axis_size("shard")
+    every = tokens.shape[0] * shards * lax.axis_size("expert")
+    if every > DENSE_TOKENS or rel_bias.shape[1] % shards or tokens.shape[0] % TILE:
+        return routed_plan(*arguments)
+    return dense_plan(*arguments)
+
+
 def solution(mesh):
     placed = (
         P(("expert", "shard"), None),

time: 1390 us -> 930 us (0.67)
  local copies, waits for them, and re-layouts: 251 us -> 48.1 us
  matrix products: 215 us -> 29.1 us
  blocking collectives: 109 us -> 0 us
  Pallas kernels: 0 us -> 95.8 us
  other arithmetic: 71.7 us -> 36.6 us
  waiting for transfers between devices: 695 us -> 680 us
    scatter x2 -> x0, local copies, waits for them, and re-layouts: 139 us -> none  [the longest x1 69.4 us: per_device(): grad_outgoing = jnp.zeros((experts, capacity, model_width), jnp.bfloat16)...]
    reduce_scatter x7 -> x3, waiting for transfers between devices: 445 us -> 325 us  [the longest x1 158 us: dense_plan(): lax.psum_scatter(out_parts, ('expert', 'shard'), scatter_dimension=0, til...]
    pallas_call x0 -> x3, Pallas kernels: none -> 95.8 us  [the longest x1 63.2 us: run_experts(): pl.pallas_call(expert_step, grid=(blocks // group,), in_specs=[small, sma...]
    dot_general x20 -> x3, matrix products: 97.9 us -> 8.8 us  [the longest x1 8.07 us: dense_plan(): lax.dot_general(full_router, normed_all, (((0,), (2,)), ((), ())), prefer...]
    psum x1, waiting for transfers between devices: 0.01 us -> 55.7 us  [dense_plan(): final = lax.psum(final, 'expert').reshape(-1).astype(f32)]
    all_gather x4 -> x0, blocking collectives: 55.5 us -> none  [the longest x1 15.7 us: per_device(): lax.all_gather(w_router, 'shard', axis=0, tiled=True)]
    dot_general x9 -> x4, matrix products: 57.6 us -> 6.24 us  [matmul(): return jnp.dot(left_operand, right_side, preferred_element_type=jnp.float32)]
    all_gather x10 -> x5, waiting for transfers between devices: 209 us -> 259 us  [the longest x1 95.5 us: dense_plan(): normed_all = lax.all_gather(normed_two, ('expert', 'shard'), axis=0)]
  transfers between devices with their start and end apart: 23 -> 12, of which waited for: 17 -> 10; matrix products, arithmetic and copies ran while one was open for 28% -> 6% of each run, Pallas kernels for 0% -> 2%
where the time goes in v1:
time: 930 us; the launch traced here: 919 us
  waiting for transfers between devices  680 us (73%)
  Pallas kernels  95.8 us (10%)
  local copies, waits for them, and re-layouts  48.1 us (5%)
  other arithmetic  36.6 us (4%)
  matrix products  29.1 us (3%)
  between operations  14.8 us (2%)
  starting transfers between devices  14.3 us (2%)
    reduce_scatter x1, waiting for transfers between devices, dense_plan(): lax.psum_scatter(out_parts, ('expert', 'shard'), scatter_dimension=0, til...  158 us
    reduce_scatter x1, waiting for transfers between devices, dense_plan(): lax.psum_scatter(back_parts, ('expert', 'shard'), scatter_dimension=0, ti...  156 us
    all_gather x1, waiting for transfers between devices, dense_plan(): normed_all = lax.all_gather(normed_two, ('expert', 'shard'), axis=0)  95.5 us
    all_gather x1, waiting for transfers between devices, dense_plan(): closed = lax.all_gather(closing, ('expert', 'shard'), axis=0)  79.7 us
    pallas_call x1, Pallas kernels, run_experts(): pl.pallas_call(expert_step, grid=(blocks // group,), in_specs=[small, sma...  63.2 us
    psum x1, waiting for transfers between devices, dense_plan(): final = lax.psum(final, 'expert').reshape(-1).astype(f32)  55.7 us
    all_gather x1, waiting for transfers between devices, dense_plan(): opened = lax.all_gather(opening, 'shard', axis=0)  50.5 us
    all_gather x1, waiting for transfers between devices, dense_plan(): lax.all_gather(grad_hidden.astype(bf16), 'shard', axis=0, tiled=True)  33.6 us
  transfers between devices with their start and end apart: 12, of which 10 were waited for; matrix products, arithmetic and copies ran while one was open for 6% of the time, Pallas kernels for 2%

profile of v1, /device:TPU:0, one launch (start us, length us, event | category | flops | bytes accessed | tf_op | source)
XLA Modules:
  0.0 919.0 jit_solution(7424567002886454529)
XLA Ops:
  16.2 6.4 all-to-all-start
  23.7 50.5 %all-gather.13.cloned.1.call-done = bf16[1088,768]{1,0:T(8,128)(2,1)} async-done(((bf16[272,768]{1,0:T(8,128)(2,1)}), bf16[1088,768]{1,0:T(8,128)(2,1)}) %all-gather.13.cloned.1.call-update) | async-done | bytes 1671184 | tf_op jit(solution)/shard_map/all_gather | solution.py:681
  82.5 3.9 convolution_convert_fusion.qkv_ref
  86.5 17.7 %shard_map.238 = (bf16[1024,192]{1,0:T(8,128)(2,1)}, bf16[3,1024,1024]{2,1,0:T(8,128)(2,1)}) custom-call(bf16[1024,576]{1,0:T(8,128)(2,1)} %convolution_convert_fusion.qkv_ref, f32[3,4,512]{2,1,0:T(4,128)} %pad_maximum_fusion.4.skew_ref, s32[1024,1]{1,0:T(8,128)} %copy.185.seg_col_ref, s32[1,1024]{1,0:T(1,128)} %seg_row_ref.1), custom_call_target="tpu_custom_call" | custom-call | tf_op jit(solution)/shard_map/pallas_call | solution.py:722
  104.2 2.0 copy.186
  106.2 3.5 all-to-all-start.1
  109.8 15.6 %all-to-all-done.1 = bf16[4,256,192]{1,2,0:T(8,128)(2,1)S(1)} async-done(((bf16[4,256,192]{1,2,0:T(8,128)(2,1)}), bf16[4,256,192]{1,2,0:T(8,128)(2,1)S(1)}, u32[]{:S(2)}, u32[]{:S(2)}) %all-to-all-start.1) | async-done | bytes 393248 | tf_op jit(solution)/shard_map/all_to_all | solution.py:731
  128.7 79.7 %all-gather.15.cloned.1.call-done = bf16[8704,768]{1,0:T(8,128)(2,1)} async-done(((bf16[272,768]{1,0:T(8,128)(2,1)}), bf16[8704,768]{1,0:T(8,128)(2,1)}) %all-gather.15.cloned.1.call-update) | async-done | bytes 13369360 | tf_op jit(solution)/shard_map/all_gather | solution.py:700
  210.5 95.5 %all-gather.17.cloned.1.call-done = bf16[8192,768]{1,0:T(8,128)(2,1)} async-done(((bf16[256,768]{1,0:T(8,128)(2,1)}), bf16[8192,768]{1,0:T(8,128)(2,1)}) %all-gather.17.cloned.1.call-update) | async-done | bytes 12582928 | tf_op jit(solution)/shard_map/all_gather | solution.py:740
  306.0 8.1 fusion.55
  315.5 63.2 %shard_map.239 = (bf16[32,256,768]{2,1,0:T(8,128)(2,1)}, bf16[32,256,768]{2,1,0:T(8,128)(2,1)}, f32[2,32,1,256]{3,2,1,0:T(1,128)}, f32[2,768,768]{2,1,0:T(8,128)}, f32[2,768,768]{2,1,0:T(8,128)}) custom-call(f32[2,32,1,256]{3,2,1,0:T(1,128)} %broadcast_in_dim.29.ranks_ref, f32[2,32,1,256]{3,2,1,0:T(1,128)} %broadcast_in_dim.36.gates_ref, ...), custom_call_target="tpu_custom_call" | custom-call | tf_op jit(solution)/shard_map/pallas_call | solution.py:613
  379.7 11.0 %fusion.1 = bf16[32,272,768]{2,1,0:T(8,128)(2,1)} fusion(bf16[32,1,512]{2,1,0:T(2,128)(2,1)S(1)} %convert_element_type.197, bf16[32,256,768]{2,1,0:T(8,128)(2,1)} %get-tuple-element.71), kind=kLoop, calls=%fused_computation.2 | loop fusion | flops 40108032 | bytes 25985024 | tf_op jit(solution)/shard_map/concatenate | solution.py:771
  392.1 155.9 %reduce-scatter.6.cloned.1.call-done = bf16[1,272,768]{2,1,0:T(8,128)(2,1)} async-done(((bf16[32,272,768]{2,1,0:T(8,128)(2,1)}), bf16[1,272,768]{2,1,0:T(8,128)(2,1)}) %reduce-scatter.6.cloned.1.call-update) | async-done | bytes 417808 | tf_op jit(solution)/shard_map/reduce_scatter | solution.py:772
  548.8 2.4 multiply_reduce_fusion
  551.2 158.1 %reduce-scatter.4.cloned.1.call-done = bf16[1,256,768]{2,1,0:T(8,128)(2,1)} async-done(((bf16[32,256,768]{2,1,0:T(8,128)(2,1)}), bf16[1,256,768]{2,1,0:T(8,128)(2,1)}) %reduce-scatter.4.cloned.1.call-update) | async-done | bytes 393232 | tf_op jit(solution)/shard_map/reduce_scatter | solution.py:773
  709.3 2.8 fusion.49
  714.8 33.6 %all-gather.11.cloned.1.call-done = bf16[1024,768]{1,0:T(8,128)(2,1)} async-done(((bf16[256,768]{1,0:T(8,128)(2,1)}), bf16[1024,768]{1,0:T(8,128)(2,1)}) %all-gather.11.cloned.1.call-update) | async-done | bytes 1572880 | tf_op jit(solution)/shard_map/all_gather | solution.py:791
  748.4 2.1 convolution_convert_fusion.2
  751.5 14.9 %shard_map.240 = (bf16[1024,576]{1,0:T(8,128)(2,1)}, f32[3,4,512]{2,1,0:T(4,128)}) custom-call(bf16[1024,576]{1,0:T(8,128)(2,1)} %convolution_convert_fusion.qkv_ref, bf16[1024,192]{1,0:T(8,128)(2,1)} %copy.194.grad_ref, bf16[3,1024,1024]{2,1,0:T(8,128)(2,1)} %get-tuple-element.73.prob_ref), custom_call_target="tpu_custom_call" | custom-call | tf_op jit(solution)/shard_map/pallas_call | solution.py:795
  767.9 4.9 fusion.8
  778.9 2.7 convolution_convert_fusion.1
  782.7 3.6 all-to-all-start.2
  786.4 1.9 convolution_convert_fusion.3
  789.3 23.3 %all-to-all-done.2 = bf16[4,208,576]{2,1,0:T(8,128)(2,1)S(1)} async-done(((bf16[4,208,576]{2,1,0:T(8,128)(2,1)}), bf16[4,208,576]{2,1,0:T(8,128)(2,1)S(1)}, u32[]{:S(2)}, u32[]{:S(2)}) %all-to-all-start.2) | async-done | bytes 958496 | tf_op jit(solution)/shard_map/all_to_all | solution.py:848
  815.9 55.7 %all-reduce.8.cloned.1.call-done = bf16[4640,128]{1,0:T(8,128)(2,1)} async-done(((bf16[4640,128]{1,0:T(8,128)(2,1)}), bf16[4640,128]{1,0:T(8,128)(2,1)}) %all-reduce.8.cloned.1.call-update) | async-done | bytes 1187856 | tf_op jit(solution)/shard_map/psum | solution.py:863
  871.5 3.0 convert_bitcast_fusion
  874.6 3.1 reshape.404
  877.7 6.3 fusion.51
  885.5 2.4 squeeze.22
  889.3 2.4 squeeze.23
  898.1 10.6 %reduce-scatter.8.cloned.1.call-done = bf16[256,768]{1,0:T(8,128)(2,1)} async-done(((bf16[1024,768]{1,0:T(8,128)(2,1)}), bf16[256,768]{1,0:T(8,128)(2,1)}) %reduce-scatter.8.cloned.1.call-update) | async-done | bytes 393232 | tf_op jit(solution)/shard_map/reduce_scatter | solution.py:809
  910.0 2.0 fusion.22
  (189 shorter events, 55.4 us)
Async XLA Ops:
  7.2 6.0 copy-start.13
  7.2 6.1 copy-start.5
  7.2 6.9 copy-start.10
  7.2 67.0 %all-gather.13.cloned.1.call-start = ((), (), s32[]{:S(2)}) async-start(), calls=%async_computation.12 | async-start | bytes 2088960 | tf_op jit(solution)/shard_map/all_gather | solution.py:681
  10.5 3.8 copy-start.11
  12.3 2.1 copy-start.12
  12.4 97.4 %all-gather.9.cloned.1.call-start = ((), (), s32[]{:S(2)}) async-start(), calls=%async_computation.6 | async-start | bytes 1474560 | tf_op jit(solution)/shard_map/all_gather | solution.py:695
  13.1 195.3 %all-gather.15.cloned.1.call-start = ((), (), s32[]{:S(2)}) async-start(), calls=%async_computation.13 | async-start | bytes 13787136 | tf_op jit(solution)/shard_map/all_gather | solution.py:700
  14.9 7.8 copy-start.14
  16.2 59.3 %copy-start.16 = (s32[1024]{0:T(1024)S(1)}, s32[1024]{0:T(1024)}, u32[]{:S(2)}) copy-start(s32[1024]{0:T(1024)} %param.37) | copy-start | bytes 12292
  16.2 65.4 %all-to-all-start = ((bf16[4,192,576]{2,1,0:T(8,128)(2,1)}), bf16[4,192,576]{2,1,0:T(8,128)(2,1)S(1)}, u32[]{:S(2)}, u32[]{:S(2)}) async-start(bf16[4,192,576]{2,1,0:T(8,128)(2,1)} %copy.180), calls=%async_computation | async-start | bytes 1966080 | tf_op jit(solution)/shard_map/all_to_all | solution.py:693
  74.2 5.8 copy-start.1
  81.6 0.9 copy-start.7
  86.5 38.8 %copy-start.2 = (bf16[256,768]{1,0:T(8,128)(2,1)S(1)}, bf16[256,768]{1,0:T(8,128)(2,1)}, u32[]{:S(2)}) copy-start(bf16[256,768]{1,0:T(8,128)(2,1)} %param.23) | copy-start | bytes 1179652
  106.2 19.2 %all-to-all-start.1 = ((bf16[4,256,192]{1,2,0:T(8,128)(2,1)}), bf16[4,256,192]{1,2,0:T(8,128)(2,1)S(1)}, u32[]{:S(2)}, u32[]{:S(2)}) async-start(bf16[4,256,192]{1,2,0:T(8,128)(2,1)} %copy.186), calls=%async_computation.1 | async-start | bytes 786432 | tf_op jit(solution)/shard_map/all_to_all | solution.py:731
  109.6 196.4 %all-gather.17.cloned.1.call-start = ((), (), s32[]{:S(2)}) async-start(), calls=%async_computation.14 | async-start | bytes 12976128 | tf_op jit(solution)/shard_map/all_gather | solution.py:740
  128.1 419.9 %reduce-scatter.6.cloned.1.call-start = ((), (), s32[]{:S(2)}) async-start(), calls=%async_computation.8 | async-start | bytes 13787136 | tf_op jit(solution)/shard_map/reduce_scatter | solution.py:772
  390.7 318.5 %reduce-scatter.4.cloned.1.call-start = ((), (), s32[]{:S(2)}) async-start(), calls=%async_computation.7 | async-start | bytes 12976128 | tf_op jit(solution)/shard_map/reduce_scatter | solution.py:773
  390.8 1.0 copy-start.3
  391.3 357.1 %all-gather.11.cloned.1.call-start = ((), (), s32[]{:S(2)}) async-start(), calls=%async_computation.9 | async-start | bytes 1966080 | tf_op jit(solution)/shard_map/all_gather | solution.py:791
  709.3 4.9 copy-start.15
  751.5 16.4 %copy-start.8 = (bf16[4,192,576]{2,1,0:T(8,128)(2,1)S(1)}, bf16[4,192,576]{2,1,0:T(8,128)(2,1)}, u32[]{:S(2)}) copy-start(bf16[4,192,576]{2,1,0:T(8,128)(2,1)} %copy-done.7) | copy-start | bytes 2654212
  767.9 8.4 copy-start.17
  782.7 3.7 copy-start.9
  782.7 29.9 %all-to-all-start.2 = ((bf16[4,208,576]{2,1,0:T(8,128)(2,1)}), bf16[4,208,576]{2,1,0:T(8,128)(2,1)S(1)}, u32[]{:S(2)}, u32[]{:S(2)}) async-start(bf16[4,208,576]{2,1,0:T(8,128)(2,1)} %pad_maximum_fusion.1), calls=%async_computation.5 | async-start | bytes 2129920 | tf_op jit(solution)/shard_map/all_to_all | solution.py:848
  786.4 85.2 %all-reduce.8.cloned.1.call-start = ((), (), s32[]{:S(2)}) async-start(), calls=%async_computation.11 | async-start | bytes 2375680 | tf_op jit(solution)/shard_map/psum | solution.py:863
  813.0 1.0 copy-start.6
  815.1 93.6 %reduce-scatter.8.cloned.1.call-start = ((), (), s32[]{:S(2)}) async-start(), calls=%async_computation.10 | async-start | bytes 1966080 | tf_op jit(solution)/shard_map/reduce_scatter | solution.py:809
  871.5 3.0 copy-start
  893.5 16.5 %copy-start.4 = (f32[256,768]{1,0:T(8,128)S(1)}, f32[256,768]{1,0:T(8,128)}, u32[]{:S(2)}) copy-start(f32[256,768]{1,0:T(8,128)} %get-tuple-element.157) | copy-start | bytes 2359300
Sparse Core Ops, SparseCore 0:
  12.5 61.7 all-gather.12
  75.8 29.5 all-gather.8
  108.8 99.5 all-gather.14
  211.7 94.1 all-gather.16
  390.8 157.1 reduce-scatter.5
  554.9 154.3 reduce-scatter.3
  712.2 36.1 all-gather.10
  815.3 56.2 all-reduce.7
  874.0 34.7 reduce-scatter.7

commit v2 on v1

--- a/solution.py
+++ b/solution.py
@@ -690,9 +690,12 @@
 
     stacked = jnp.stack([w_query, w_key, w_value], axis=1).reshape(part_rows, 3, shards, owned)
     stacked = stacked.transpose(2, 0, 1, 3).reshape(shards, part_rows, 3 * owned)
-    own_qkv = lax.all_to_all(stacked, "shard", split_axis=0, concat_axis=0, tiled=True)
-    own_qkv = own_qkv.reshape(width, 3 * owned)
-    full_proj = lax.all_gather(w_out_attn, "shard", axis=0, tiled=True)
+    copies = jnp.broadcast_to(w_out_attn[None], (shards,) + w_out_attn.shape)
+    weights = lax.all_to_all(
+        jnp.concatenate([stacked, copies], axis=2), "shard", split_axis=0, concat_axis=0, tiled=True
+    )
+    own_qkv = weights[:, :, : 3 * owned].reshape(width, 3 * owned)
+    full_proj = weights[:, :, 3 * owned :].reshape(width, width)
 
     closing = jnp.concatenate(
         [out_grad, pad_rows(routes.T.reshape(-1).astype(bf16), PACK_ROWS, width)], axis=0
@@ -770,8 +773,6 @@
     )
     back_parts = jnp.concatenate([back_parts, dots_rows], axis=1)
     back_here = lax.psum_scatter(back_parts, ("expert", "shard"), scatter_dimension=0, tiled=True)[0]
-    out_here = lax.psum_scatter(out_parts, ("expert", "shard"), scatter_dimension=0, tiled=True)[0]
-    layer_out = (hidden + out_here.astype(f32)).astype(bf16)
 
     router = jax.nn.softmax(matmul(normed_two, full_router), axis=-1)
     route_onehot = (routes[:, :, None] == expert_ids[None, None, :]).astype(f32)
@@ -789,6 +790,10 @@
     grad_norm_two, grad_gain_two = norm_back(hidden, inverse_two, gain_two, grad_normed_two)
     grad_hidden = out_grad.astype(f32) + grad_norm_two
     grad_branch = lax.all_gather(grad_hidden.astype(bf16), "shard", axis=0, tiled=True)
+
+    out_parts, grad_branch = lax.optimization_barrier((out_parts, grad_branch))
+    out_here = lax.psum_scatter(out_parts, ("expert", "shard"), scatter_dimension=0, tiled=True)[0]
+    layer_out = (hidden + out_here.astype(f32)).astype(bf16)
 
     grad_w_proj = contract_first(mixed, grad_branch)
     grad_mixed = contract_last(grad_branch, w_out_attn).astype(bf16)

time: 930 us -> 912 us (0.981)
  waiting for transfers between devices: 680 us -> 659 us
    all_gather x1, waiting for transfers between devices: 79.7 us -> 44.5 us  [dense_plan(): closed = lax.all_gather(closing, ('expert', 'shard'), axis=0)]
    all_gather x1, waiting for transfers between devices: 50.5 us -> 62.9 us  [dense_plan(): opened = lax.all_gather(opening, 'shard', axis=0)]
  transfers between devices with their start and end apart: 12 -> 11, of which waited for: 10 -> 11; matrix products, arithmetic and copies ran while one was open for 6% -> 7% of each run, Pallas kernels for 2% -> 2%
where the time goes in v2:
time: 912 us; the launch traced here: 908 us
  waiting for transfers between devices  659 us (72%)
  Pallas kernels  95.7 us (10%)
  local copies, waits for them, and re-layouts  55.3 us (6%)
  other arithmetic  39 us (4%)
  matrix products  29.8 us (3%)
  between operations  15.2 us (2%)
  starting transfers between devices  14.4 us (2%)
    reduce_scatter x1, waiting for transfers between devices, dense_plan(): lax.psum_scatter(out_parts, ('expert', 'shard'), scatter_dimension=0, til...  157 us
    reduce_scatter x1, waiting for transfers between devices, dense_plan(): lax.psum_scatter(back_parts, ('expert', 'shard'), scatter_dimension=0, ti...  156 us
    all_gather x1, waiting for transfers between devices, dense_plan(): normed_all = lax.all_gather(normed_two, ('expert', 'shard'), axis=0)  95.7 us
    pallas_call x1, Pallas kernels, run_experts(): pl.pallas_call(expert_step, grid=(blocks // group,), in_specs=[small, sma...  63.2 us
    all_gather x1, waiting for transfers between devices, dense_plan(): opened = lax.all_gather(opening, 'shard', axis=0)  62.9 us
    psum x1, waiting for transfers between devices, dense_plan(): final = lax.psum(final, 'expert').reshape(-1).astype(f32)  54.9 us
    all_gather x1, waiting for transfers between devices, dense_plan(): closed = lax.all_gather(closing, ('expert', 'shard'), axis=0)  44.5 us
    all_gather x1, waiting for transfers between devices, dense_plan(): lax.all_gather(grad_hidden.astype(bf16), 'shard', axis=0, tiled=True)  30.1 us
  transfers between devices with their start and end apart: 11, of which 11 were waited for; matrix products, arithmetic and copies ran while one was open for 7% of the time, Pallas kernels for 2%

profile of v2, /device:TPU:0, one launch (start us, length us, event | category | flops | bytes accessed | tf_op | source)
XLA Modules:
  0.0 908.1 jit_solution(10921213895602549858)
XLA Ops:
  16.5 2.1 pad_maximum_fusion
  18.6 6.9 all-to-all-start
  26.5 62.9 %all-gather.10.cloned.1.call-done = bf16[1088,768]{1,0:T(8,128)(2,1)} async-done(((bf16[272,768]{1,0:T(8,128)(2,1)}), bf16[1088,768]{1,0:T(8,128)(2,1)}) %all-gather.10.cloned.1.call-update) | async-done | bytes 1671184 | tf_op jit(solution)/shard_map/all_gather | solution.py:681
  96.8 3.2 all-to-all-done
  102.2 3.9 convolution_convert_fusion.qkv_ref
  106.1 17.7 %shard_map.238 = (bf16[1024,192]{1,0:T(8,128)(2,1)}, bf16[3,1024,1024]{2,1,0:T(8,128)(2,1)}) custom-call(bf16[1024,576]{1,0:T(8,128)(2,1)} %convolution_convert_fusion.qkv_ref, f32[3,4,512]{2,1,0:T(4,128)} %pad_maximum_fusion.5.skew_ref, s32[1024,1]{1,0:T(8,128)} %copy.156.seg_col_ref, s32[1,1024]{1,0:T(1,128)} %seg_row_ref.1), custom_call_target="tpu_custom_call" | custom-call | tf_op jit(solution)/shard_map/pallas_call | solution.py:725
  125.7 3.5 all-to-all-start.1
  129.3 19.6 %all-to-all-done.1 = bf16[4,256,192]{1,2,0:T(8,128)(2,1)S(1)} async-done(((bf16[4,256,192]{1,2,0:T(8,128)(2,1)}), bf16[4,256,192]{1,2,0:T(8,128)(2,1)S(1)}, u32[]{:S(2)}, u32[]{:S(2)}) %all-to-all-start.1) | async-done | bytes 393248 | tf_op jit(solution)/shard_map/all_to_all | solution.py:734
  149.0 2.1 multiply_reduce_fusion.2
  153.0 44.5 %all-gather.12.cloned.1.call-done = bf16[8704,768]{1,0:T(8,128)(2,1)} async-done(((bf16[272,768]{1,0:T(8,128)(2,1)}), bf16[8704,768]{1,0:T(8,128)(2,1)}) %all-gather.12.cloned.1.call-update) | async-done | bytes 13369360 | tf_op jit(solution)/shard_map/all_gather | solution.py:703
  199.6 95.7 %all-gather.14.cloned.1.call-done = bf16[8192,768]{1,0:T(8,128)(2,1)} async-done(((bf16[256,768]{1,0:T(8,128)(2,1)}), bf16[8192,768]{1,0:T(8,128)(2,1)}) %all-gather.14.cloned.1.call-update) | async-done | bytes 12582928 | tf_op jit(solution)/shard_map/all_gather | solution.py:743
  295.2 8.0 fusion.56
  304.6 63.2 %shard_map.239 = (bf16[32,256,768]{2,1,0:T(8,128)(2,1)}, bf16[32,256,768]{2,1,0:T(8,128)(2,1)}, f32[2,32,1,256]{3,2,1,0:T(1,128)}, f32[2,768,768]{2,1,0:T(8,128)}, f32[2,768,768]{2,1,0:T(8,128)}) custom-call(f32[2,32,1,256]{3,2,1,0:T(1,128)} %broadcast_in_dim.32.ranks_ref, f32[2,32,1,256]{3,2,1,0:T(1,128)} %broadcast_in_dim.39.gates_ref, ...), custom_call_target="tpu_custom_call" | custom-call | tf_op jit(solution)/shard_map/pallas_call | solution.py:613
  368.8 11.0 %fusion.1 = bf16[32,272,768]{2,1,0:T(8,128)(2,1)} fusion(bf16[32,1,512]{2,1,0:T(2,128)(2,1)S(1)} %convert_element_type.197, bf16[32,256,768]{2,1,0:T(8,128)(2,1)} %get-tuple-element.73), kind=kLoop, calls=%fused_computation.2 | loop fusion | flops 40108032 | bytes 25985024 | tf_op jit(solution)/shard_map/concatenate | solution.py:774
  381.2 156.0 %reduce-scatter.4.cloned.1.call-done = bf16[1,272,768]{2,1,0:T(8,128)(2,1)} async-done(((bf16[32,272,768]{2,1,0:T(8,128)(2,1)}), bf16[1,272,768]{2,1,0:T(8,128)(2,1)}) %reduce-scatter.4.cloned.1.call-update) | async-done | bytes 417808 | tf_op jit(solution)/shard_map/reduce_scatter | solution.py:775
  538.0 2.1 multiply_reduce_fusion
  548.3 30.1 %all-gather.8.cloned.1.call-done = bf16[1024,768]{1,0:T(8,128)(2,1)} async-done(((bf16[256,768]{1,0:T(8,128)(2,1)}), bf16[1024,768]{1,0:T(8,128)(2,1)}) %all-gather.8.cloned.1.call-update) | async-done | bytes 1572880 | tf_op jit(solution)/shard_map/all_gather | solution.py:792
  578.4 2.1 convolution_convert_fusion.2
  581.4 14.8 %shard_map.240 = (bf16[1024,576]{1,0:T(8,128)(2,1)}, f32[3,4,512]{2,1,0:T(4,128)}) custom-call(bf16[1024,576]{1,0:T(8,128)(2,1)} %convolution_convert_fusion.qkv_ref, bf16[1024,192]{1,0:T(8,128)(2,1)} %copy.165.grad_ref, bf16[3,1024,1024]{2,1,0:T(8,128)(2,1)} %get-tuple-element.77.prob_ref), custom_call_target="tpu_custom_call" | custom-call | tf_op jit(solution)/shard_map/pallas_call | solution.py:800
  597.8 5.2 fusion.8
  609.1 2.7 convolution_convert_fusion.1
  612.9 3.5 all-to-all-start.2
  618.7 24.0 %all-to-all-done.2 = bf16[4,208,576]{2,1,0:T(8,128)(2,1)S(1)} async-done(((bf16[4,208,576]{2,1,0:T(8,128)(2,1)}), bf16[4,208,576]{2,1,0:T(8,128)(2,1)S(1)}, u32[]{:S(2)}, u32[]{:S(2)}) %all-to-all-start.2) | async-done | bytes 958496 | tf_op jit(solution)/shard_map/all_to_all | solution.py:853
  646.7 54.9 %all-reduce.8.cloned.1.call-done = bf16[4640,128]{1,0:T(8,128)(2,1)} async-done(((bf16[4640,128]{1,0:T(8,128)(2,1)}), bf16[4640,128]{1,0:T(8,128)(2,1)}) %all-reduce.8.cloned.1.call-update) | async-done | bytes 1187856 | tf_op jit(solution)/shard_map/psum | solution.py:868
  702.8 3.1 reshape.403
  705.9 6.3 fusion.53
  713.7 2.4 squeeze.22
  717.5 2.5 squeeze.23
  721.4 2.4 squeeze.24
  729.3 9.3 %reduce-scatter.8.cloned.1.call-done = bf16[256,768]{1,0:T(8,128)(2,1)} async-done(((bf16[1024,768]{1,0:T(8,128)(2,1)}), bf16[256,768]{1,0:T(8,128)(2,1)}) %reduce-scatter.8.cloned.1.call-update) | async-done | bytes 393232 | tf_op jit(solution)/shard_map/reduce_scatter | solution.py:814
  739.9 2.0 fusion.23
  742.0 157.1 %reduce-scatter.6.cloned.1.call-done = bf16[1,256,768]{2,1,0:T(8,128)(2,1)} async-done(((bf16[32,256,768]{2,1,0:T(8,128)(2,1)}), bf16[1,256,768]{2,1,0:T(8,128)(2,1)}) %reduce-scatter.6.cloned.1.call-update) | async-done | bytes 393232 | tf_op jit(solution)/shard_map/reduce_scatter | solution.py:795
  (194 shorter events, 68.2 us)
Async XLA Ops:
  7.2 7.7 copy-start.9
  7.2 7.9 copy-start.10
  7.2 8.1 copy-start.11
  7.2 82.2 %all-gather.10.cloned.1.call-start = ((), (), s32[]{:S(2)}) async-start(), calls=%async_computation.11 | async-start | bytes 2088960 | tf_op jit(solution)/shard_map/all_gather | solution.py:681
  12.3 185.2 %all-gather.12.cloned.1.call-start = ((), (), s32[]{:S(2)}) async-start(), calls=%async_computation.12 | async-start | bytes 13787136 | tf_op jit(solution)/shard_map/all_gather | solution.py:703
  15.5 1.0 copy-start.12
  18.6 6.9 copy-start.17
  18.6 72.2 %copy-start.18 = (s32[1024]{0:T(1024)S(1)}, s32[1024]{0:T(1024)}, u32[]{:S(2)}) copy-start(s32[1024]{0:T(1024)} %param.37) | copy-start | bytes 12292
  18.6 81.4 %all-to-all-start = ((bf16[4,192,1344]{2,1,0:T(8,128)(2,1)}), bf16[4,192,1344]{2,1,0:T(8,128)(2,1)}, u32[]{:S(2)}, u32[]{:S(2)}) async-start(bf16[4,192,1344]{2,1,0:T(8,128)(2,1)} %pad_maximum_fusion), calls=%async_computation | async-start | bytes 4325376 | tf_op jit(solution)/shard_map/all_to_all | solution.py:694
  89.4 5.8 copy-start.1
  101.3 0.9 copy-start.7
  106.1 42.9 %copy-start.3 = (bf16[256,768]{1,0:T(8,128)(2,1)S(1)}, bf16[256,768]{1,0:T(8,128)(2,1)}, u32[]{:S(2)}) copy-start(bf16[256,768]{1,0:T(8,128)(2,1)} %param.23) | copy-start | bytes 1179652
  125.7 23.2 %all-to-all-start.1 = ((bf16[4,256,192]{1,2,0:T(8,128)(2,1)}), bf16[4,256,192]{1,2,0:T(8,128)(2,1)S(1)}, u32[]{:S(2)}, u32[]{:S(2)}) async-start(bf16[4,256,192]{1,2,0:T(8,128)(2,1)} %copy.157), calls=%async_computation.1 | async-start | bytes 786432 | tf_op jit(solution)/shard_map/all_to_all | solution.py:734
  129.2 166.0 %all-gather.14.cloned.1.call-start = ((), (), s32[]{:S(2)}) async-start(), calls=%async_computation.13 | async-start | bytes 12976128 | tf_op jit(solution)/shard_map/all_gather | solution.py:743
  151.7 386.4 %copy-start.16 = (f32[256]{0:T(256)}, f32[256]{0:T(256)S(1)}, u32[]{:S(2)}) copy-start(f32[256]{0:T(256)S(1)} %get-tuple-element.181) | copy-start | bytes 3076
  152.6 384.6 %reduce-scatter.4.cloned.1.call-start = ((), (), s32[]{:S(2)}) async-start(), calls=%async_computation.6 | async-start | bytes 13787136 | tf_op jit(solution)/shard_map/reduce_scatter | solution.py:775
  379.8 1.0 copy-start.2
  379.8 1.3 copy-start.15
  379.9 198.5 %all-gather.8.cloned.1.call-start = ((), (), s32[]{:S(2)}) async-start(), calls=%async_computation.7 | async-start | bytes 1966080 | tf_op jit(solution)/shard_map/all_gather | solution.py:792
  537.9 2.2 copy-start.6
  540.1 38.3 %copy-start.13 = (bf16[192,768]{1,0:T(8,128)(2,1)S(1)}, bf16[192,768]{1,0:T(8,128)(2,1)}, u32[]{:S(2)}) copy-start(bf16[192,768]{1,0:T(8,128)(2,1)} %param.27) | copy-start | bytes 884740
  597.8 8.8 copy-start.19
  597.8 9.4 %copy-start.14 = (bf16[4,3072]{1,0:T(4,128)(2,1)S(1)}, bf16[4,3072]{1,0:T(4,128)(2,1)}, u32[]{:S(2)}) copy-start(bf16[4,3072]{1,0:T(4,128)(2,1)} %reshape.389) | copy-start | bytes 73732
  611.9 4.7 copy-start.8
  612.9 29.7 %all-to-all-start.2 = ((bf16[4,208,576]{2,1,0:T(8,128)(2,1)}), bf16[4,208,576]{2,1,0:T(8,128)(2,1)S(1)}, u32[]{:S(2)}, u32[]{:S(2)}) async-start(bf16[4,208,576]{2,1,0:T(8,128)(2,1)} %pad_maximum_fusion.2), calls=%async_computation.5 | async-start | bytes 2129920 | tf_op jit(solution)/shard_map/all_to_all | solution.py:853
  616.5 85.1 %all-reduce.8.cloned.1.call-start = ((), (), s32[]{:S(2)}) async-start(), calls=%async_computation.10 | async-start | bytes 2375680 | tf_op jit(solution)/shard_map/psum | solution.py:868
  645.2 93.5 %reduce-scatter.8.cloned.1.call-start = ((), (), s32[]{:S(2)}) async-start(), calls=%async_computation.9 | async-start | bytes 1966080 | tf_op jit(solution)/shard_map/reduce_scatter | solution.py:814
  645.9 253.1 %reduce-scatter.6.cloned.1.call-start = ((), (), s32[]{:S(2)}) async-start(), calls=%async_computation.8 | async-start | bytes 12976128 | tf_op jit(solution)/shard_map/reduce_scatter | solution.py:795
  717.5 6.4 copy-start
  725.6 14.3 %copy-start.4 = (f32[256,768]{1,0:T(8,128)S(1)}, f32[256,768]{1,0:T(8,128)}, u32[]{:S(2)}) copy-start(f32[256,768]{1,0:T(8,128)} %get-tuple-element.149) | copy-start | bytes 2359300
  725.7 1.4 copy-start.5
Sparse Core Ops, SparseCore 0:
  12.4 76.9 all-gather.9
  92.8 104.7 all-gather.11
  201.0 94.1 all-gather.13
  380.0 157.1 reduce-scatter.3
  542.3 36.0 all-gather.7
  645.3 56.2 all-reduce.7
  703.9 34.7 reduce-scatter.7
  744.7 154.3 reduce-scatter.5
